TPU v7x, 32 devices: a whole 2x2x4 slice. The times are simulated.
32 devices in a mesh: spec: 8 (over y, x, core), tile: 4 (over z).
Axes of the slice: x: 2, y: 2, z: 4, core: 2. Of those that a mesh axis runs over, the one named last changes fastest.
Arguments:
- spectrum: float32 [1152, 16, 512], P('spec', None, 'tile'), may hold values from 0.1 to 2
- depth_speed: float32 [16, 512], P(None, 'tile'), may hold values from 0.5 to 1
- turning: float32 [16, 512], P(None, 'tile'), may hold values from -0.5 to 0.5
- drift: float32 [1152], replicated, may hold values from -0.4 to 0.4
- partners: int32 [2, 1152], replicated, may hold values from 0 to 1151, as said below
- sea_slots: int32 [8, 4, 192], P(None, 'tile'), may hold values from 0 to 255, as said below
- sea_counts: int32 [8, 4], P(None, 'tile'), may hold values from 64 to 192
Outputs:
- new_spectrum: float32 [1152, 16, 512], P(None, 'spec', 'tile')
Inputs may be any that keep to these rules, and one draw needn't show every extreme that they name: partners[0, k] and partners[1, k] for k = f * 36 + d are components of frequency min(f + a_f, 31) and max(f - b_f, 0) and directions (d + c_f) and (d - e_f) modulo 36, with a_f, b_f, c_f, e_f between 1 and 3 and fixed for each frequency. sea_slots[j, t] names 192 distinct cells of block (j, t); its first sea_counts[j, t] entries are the block's sea cells, the others are land cells.
All inputs are finite; a program needn't handle non-finite values.
Results may differ from a plain program's by a relative error of at most 0.000075.
Values sent between devices are 32-bit elements; how exact they have to be, the bound alone decides.
A program may use at most 64 MiB of HBM per device.

v0:
```python
import jax
import jax.numpy as jnp
from jax import lax
from jax.sharding import PartitionSpec as P

ND = 36
NF = 32


speed_top = 0.6
decline = 0.0953102
dia_coeff = 0.25


def extended(cells, sides, width):
    for axis, dim in sides:
        count = lax.axis_size(axis)
        head = lax.slice_in_dim(cells, 0, width, axis=dim)
        tail = lax.slice_in_dim(cells, cells.shape[dim] - width, cells.shape[dim], axis=dim)
        cells = jnp.concatenate(
            [
                lax.ppermute(tail, axis, [(i, (i + 1) % count) for i in range(count)]),
                cells,
                lax.ppermute(head, axis, [((i + 1) % count, i) for i in range(count)]),
            ],
            axis=dim,
        )
    return cells


def sea_cells(sea_list, sea_total, per_block):
    cell_ids = jnp.arange(per_block, dtype=jnp.int32)
    slot_rank = jnp.arange(sea_list.shape[1], dtype=jnp.int32)
    is_live = slot_rank[None, :] < sea_total[:, None]
    matches = (sea_list[:, :, None] == cell_ids[None, None, :]) & is_live[:, :, None]
    return jnp.any(matches, axis=1).astype(jnp.float32)


def advect_space(energy_ext, depth_ext, speeds, cosines, sine_part, sea_mask):
    east_rate = (speeds * cosines)[:, None, None] * depth_ext[None]
    north_rate = (speeds * sine_part)[:, None, None] * depth_ext[None, :, 1:-1]
    centre = energy_ext[:, :, 1:-1]
    east_mid = east_rate[:, :, 1:-1]
    inflow = (
        jnp.maximum(east_rate[:, :, :-2], 0.0) * energy_ext[:, :, :-2]
        + jnp.maximum(-east_rate[:, :, 2:], 0.0) * energy_ext[:, :, 2:]
    )
    empty_row = jnp.zeros_like(centre[:, :1])
    from_south = jnp.concatenate(
        [empty_row, (jnp.maximum(north_rate, 0.0) * centre)[:, :-1]], axis=1
    )
    from_north = jnp.concatenate(
        [(jnp.maximum(-north_rate, 0.0) * centre)[:, 1:], empty_row], axis=1
    )
    updated = (
        centre
        - (jnp.abs(east_mid) + jnp.abs(north_rate)) * centre
        + inflow
        + from_south
        + from_north
    )
    return updated * sea_mask


def advect_direction(energy, turning):
    turn_plus = jnp.maximum(turning, 0.0)
    behind = jnp.maximum(-turning, 0.0)
    return (
        energy
        - jnp.abs(turning) * energy
        + turn_plus * jnp.roll(energy, 1, axis=1)
        + behind * jnp.roll(energy, -1, axis=1)
    )


def advect_frequency(energy, drift, n_freq, n_dir):
    shaped = energy.reshape(n_freq, n_dir, -1)
    drift_rate = drift.reshape(n_freq, n_dir, 1)
    upward = jnp.maximum(drift_rate, 0.0) * shaped
    downward = jnp.maximum(-drift_rate, 0.0) * shaped
    empty_row = jnp.zeros_like(shaped[:1])
    from_below = jnp.concatenate([empty_row, upward[:-1]], axis=0)
    from_above = jnp.concatenate([downward[1:], empty_row], axis=0)
    return (shaped - jnp.abs(drift_rate) * shaped + from_below + from_above).reshape(energy.shape)


def pick_rows(lookup_ids, values):
    return jnp.take(values, lookup_ids, axis=0)


def spread_rows(lookup_ids, values):
    return jax.ops.segment_sum(values, lookup_ids, num_segments=values.shape[0])


def shards(spectrum, depth_speed, turning, drift, partners, sea_slots, sea_counts):
    channels, grid_rows, grid_cols = spectrum.shape
    n_spec = lax.axis_size("spec")
    sub_rows = grid_rows // n_spec
    per_block = sub_rows * grid_cols
    sea_list = sea_slots[:, 0, :]
    sea_mask = sea_cells(sea_list, sea_counts[:, 0], per_block).reshape(grid_rows, grid_cols)
    energy = spectrum * sea_mask
    stacked = jnp.concatenate([energy, depth_speed[None]], axis=0)
    padded = extended(stacked, (("tile", 2),), 1)
    local_freq = channels // ND
    freq_ids = (
        lax.axis_index("spec") * local_freq + jnp.arange(local_freq, dtype=jnp.int32)
    ).astype(jnp.float32)
    speeds = jnp.repeat(speed_top * jnp.exp(-decline * freq_ids), ND)
    angles = 2.0 * jnp.pi * jnp.arange(ND, dtype=jnp.float32) / ND
    cosines = jnp.tile(jnp.cos(angles), local_freq)
    sine_part = jnp.tile(jnp.sin(angles), local_freq)
    spaced = advect_space(padded[:channels], padded[channels], speeds, cosines, sine_part, sea_mask)
    turned = advect_direction(spaced.reshape(local_freq, ND, grid_rows, grid_cols), turning)
    turned = turned.reshape(channels, grid_rows, grid_cols)
    points = lax.all_to_all(turned, "spec", split_axis=1, concat_axis=0, tiled=True)
    n_comps, point_rows, item_count = points.shape
    flattened = points.reshape(n_comps, point_rows * item_count)
    shifted = advect_frequency(flattened, drift, NF, ND)
    plus_values = pick_rows(partners[0], shifted)
    minus_values = pick_rows(partners[1], shifted)
    quartet = (
        shifted * shifted * (plus_values + minus_values)
        - 2.0 * shifted * plus_values * minus_values
    )
    source = spread_rows(partners[0], quartet) + spread_rows(partners[1], quartet) - 2.0 * quartet
    return (shifted + dia_coeff * source).reshape(n_comps, point_rows, item_count)


def solution(mesh):
    return jax.shard_map(
        shards,
        mesh=mesh,
        in_specs=(
            P("spec", None, "tile"),
            P(None, "tile"),
            P(None, "tile"),
            P(),
            P(),
            P(None, "tile", None),
            P(None, "tile"),
        ),
        out_specs=P(None, "spec", "tile"),
        check_vma=False,
    )
```

profile of v0, /device:TPU:0, one launch (start us, length us, event | category | flops | bytes accessed | tf_op | source)
XLA Modules:
  0.0 78.5 jit_solution(5284256169219370879)
XLA Ops:
  0.0 0.7 copy.37
  0.7 0.7 iota_compare_fusion.1
  2.0 1.4 %broadcast_multiply_fusion.2 = f32[144,16,128]{2,1,0:T(8,128)S(1)} fusion(f32[144,16,128]{2,1,0:T(8,128)} %param.9, f32[16,128]{1,0:T(8,128)S(1)} %reshape.114), kind=kLoop, calls=%fused_computation.52 | loop fusion | flops 294912 | bytes 2367488 | tf_op jit(solution)/shard_map/mul | solution.py:102
  3.8 1.3 %copy.25 = f32[145,16,1]{0,1,2:T(8,128)} copy(f32[145,16,1]{2,1,0:T(8,128)S(1)} %get-tuple-element.12) | data formatting | bytes 18560 | tf_op jit(solution)/shard_map/slice | solution.py:19
  5.1 3.0 %collective-permute-start = (f32[145,16,1]{0,1,2:T(8,128)}, f32[145,16,1]{0,1,2:T(8,128)S(1)}, u32[]{:S(2)}, u32[]{:S(2)}) collective-permute-start(f32[145,16,1]{0,1,2:T(8,128)} %copy.25), channel_id=1, source_target_pairs={{0,1},{1,2},{2,3},{3,0},{4,5},{5,6},{6,7},{7,4},{8,9},{9,10},{10,1... | collective-permute-start | bytes 27848 | tf_op jit(solution)/shard_map/ppermute | solution.py:22
  8.1 0.7 copy.26
  8.8 2.1 %collective-permute-start.1 = (f32[145,16,1]{0,1,2:T(8,128)S(1)}, f32[145,16,1]{0,1,2:T(8,128)}, u32[]{:S(2)}, u32[]{:S(2)}) collective-permute-start(f32[145,16,1]{0,1,2:T(8,128)S(1)} %copy.26), channel_id=1, source_target_pairs={{1,0},{2,1},{3,2},{0,3},{5,4},{6,5},{7,6},{4,7},{9,8},{10,9},{11,1... | collective-permute-start | bytes 27848 | tf_op jit(solution)/shard_map/ppermute | solution.py:24
  11.6 0.7 mul.175
  12.3 0.7 mul.169
  13.0 0.8 %copy.27 = f32[145,16,1]{2,1,0:T(8,128)S(1)} copy(f32[145,16,1]{0,1,2:T(8,128)S(1)} %collective-permute-done) | data formatting | bytes 18560 | tf_op jit(solution)/shard_map/ppermute | solution.py:22
  13.8 1.6 %copy.28 = f32[145,16,1]{2,1,0:T(8,128)S(1)} copy(f32[145,16,1]{0,1,2:T(8,128)} %collective-permute-done.1) | data formatting | bytes 18560 | tf_op jit(solution)/shard_map/ppermute | solution.py:24
  15.4 0.8 fusion.20
  17.9 2.5 %fusion.7 = f32[144,16,128]{2,1,0:T(8,128)S(1)} fusion(f32[144,16,128]{2,1,0:T(8,128)S(1)} %broadcast_multiply_fusion.2, f32[145,16,1]{2,1,0:T(8,128)S(1)} %copy.28, f32[1,16,128]{2,1,0:T(8,128)S(1)} %bitcast.27, f32[144,16,130]{2,1,0:T(8,128)S(1)} %broadcast_multiply_fusion, f32[145,16,1]{2,1,0:T(8,128)S(1)} %copy.27, ...), kind=kLoop, calls=%fused_computation.19 | loop fusion | flops 5898240 | bytes 8153792 | tf_op jit(solution)/shard_map/mul | solution.py:62
  21.7 1.4 %copy.31 = f32[144,16,128]{2,0,1:T(8,128)} copy(f32[144,16,128]{2,1,0:T(8,128)S(1)} %fusion.9) | data formatting | bytes 2359296 | tf_op jit(solution)/shard_map/add | solution.py:69
  23.1 4.1 %all-to-all-start = ((f32[144,16,128]{2,0,1:T(8,128)}), f32[144,16,128]{2,0,1:T(8,128)S(1)}, u32[]{:S(2)}, u32[]{:S(2)}) async-start(f32[144,16,128]{2,0,1:T(8,128)} %copy.31), calls=%async_computation | async-start | bytes 2359296 | tf_op jit(solution)/shard_map/all_to_all | solution.py:116
  28.7 15.2 %all-to-all-done = f32[144,16,128]{2,0,1:T(8,128)S(1)} async-done(((f32[144,16,128]{2,0,1:T(8,128)}), f32[144,16,128]{2,0,1:T(8,128)S(1)}, u32[]{:S(2)}, u32[]{:S(2)}) %all-to-all-start) | async-done | bytes 1179680 | tf_op jit(solution)/shard_map/all_to_all | solution.py:116
  44.6 0.9 %reshape_reshape.3 = f32[32,36,256]{2,1,0:T(8,128)S(1)} reshape(f32[8,144,2,128]{3,2,1,0:T(2,128)S(1)} %bitcast.24) | data formatting | bytes 2359296 | tf_op jit(solution)/shard_map/reshape;reshape | solution.py:77
  46.4 3.3 %gather_fusion = f32[1152,256]{1,0:T(8,128)S(1)} fusion(f32[1152,256]{1,0:T(8,128)S(1)} %reshape.112, s32[2048]{0:T(1024)S(1)} %pad_clamp_fusion.1), kind=kCustom, calls=%fused_computation.clone | custom fusion | bytes 2363904 | tf_op jit(solution)/shard_map/jit(_take)/gather | solution.py:88
  49.7 3.7 %gather_fusion.1 = f32[1152,256]{1,0:T(8,128)S(1)} fusion(f32[1152,256]{1,0:T(8,128)S(1)} %reshape.112, s32[2048]{0:T(1024)} %pad_clamp_fusion), kind=kCustom, calls=%fused_computation.1.clone | custom fusion | bytes 2363904 | tf_op jit(solution)/shard_map/jit(_take)/gather | solution.py:88
  53.4 2.2 %multiply_subtract_fusion.3 = f32[1152,256]{1,0:T(8,128)} fusion(f32[1152,256]{1,0:T(8,128)S(1)} %reshape.112, f32[1152,256]{1,0:T(8,128)S(1)} %gather_fusion.1, f32[1152,256]{1,0:T(8,128)S(1)} %gather_fusion, pred[1152]{0:T(1024)(128)(4,1)} %get-tuple-element.30, pred[1152]{0:T(1024)(128)(4,1)} %get-tuple-element.31), kind=kLoop, calls=%fused_computation.45 | loop fusion | flops 2654208 | bytes 4720896 | tf_op jit(solution)/shard_map/sub | solution.py:123
  55.6 8.8 %scatter_custom_fusion.1 = f32[1152,256]{1,0:T(8,128)S(1)} fusion(s32[1152]{0:T(1024)S(1)} %get-tuple-element.7, f32[1152,256]{1,0:T(8,128)} %multiply_subtract_fusion.3, f32[]{:T(128)} %constant.7.clone.1), kind=kCustom, calls=%fused_computation.47 | custom fusion | flops 294912 | bytes 1180160 | tf_op jit(solution)/shard_map/scatter-add | solution.py:92
  64.4 8.8 %scatter_custom_fusion = f32[1152,256]{1,0:T(8,128)S(1)} fusion(s32[1152]{0:T(1024)S(1)} %get-tuple-element.6, f32[1152,256]{1,0:T(8,128)} %multiply_subtract_fusion.3, f32[]{:T(128)} %constant.7.clone.1), kind=kCustom, calls=%fused_computation.49 | custom fusion | flops 294912 | bytes 1180160 | tf_op jit(solution)/shard_map/scatter-add | solution.py:92
  73.1 2.6 %multiply_add_fusion = f32[1152,256]{1,0:T(8,128)} fusion(f32[1152,256]{1,0:T(8,128)S(1)} %reshape.112, f32[1152,256]{1,0:T(8,128)} %multiply_subtract_fusion.3, f32[1152,256]{1,0:T(8,128)S(1)} %scatter_custom_fusion, f32[1152,256]{1,0:T(8,128)S(1)} %scatter_custom_fusion.1), kind=kLoop, calls=%fused_computation.44 | loop fusion | flops 1474560 | bytes 5898240 | tf_op jit(solution)/shard_map/add | solution.py:127
  75.8 2.8 %reshape.113 = f32[1152,2,128]{2,1,0:T(2,128)} reshape(f32[1152,256]{1,0:T(8,128)} %multiply_add_fusion) | data formatting | bytes 2359296 | tf_op jit(solution)/shard_map/reshape | solution.py:127
  (57 shorter events, 7.6 us)
Async XLA Ops:
  2.0 1.4 %copy-start.2 = (f32[16,128]{1,0:T(8,128)}, f32[16,128]{1,0:T(8,128)S(1)}, u32[]{:S(2)}) copy-start(f32[16,128]{1,0:T(8,128)S(1)} %reshape.114) | copy-start | bytes 24580
  2.0 1.4 %copy-start = (f32[16,128]{1,0:T(8,128)S(1)}, f32[16,128]{1,0:T(8,128)}, u32[]{:S(2)}) copy-start(f32[16,128]{1,0:T(8,128)} %param.10) | copy-start | bytes 24580
  5.1 5.8 %copy-start.9 = (f32[16,128]{1,0:T(8,128)S(1)}, f32[16,128]{1,0:T(8,128)}, u32[]{:S(2)}) copy-start(f32[16,128]{1,0:T(8,128)} %param.11) | copy-start | bytes 24580
  5.1 7.9 %collective-permute-start = (f32[145,16,1]{0,1,2:T(8,128)}, f32[145,16,1]{0,1,2:T(8,128)S(1)}, u32[]{:S(2)}, u32[]{:S(2)}) collective-permute-start(f32[145,16,1]{0,1,2:T(8,128)} %copy.25), channel_id=1, source_target_pairs={{0,1},{1,2},{2,3},{3,0},{4,5},{5,6},{6,7},{7,4},{8,9},{9,10},{10,1... | collective-permute-start | bytes 27848 | tf_op jit(solution)/shard_map/ppermute | solution.py:22
  8.8 5.0 %collective-permute-start.1 = (f32[145,16,1]{0,1,2:T(8,128)S(1)}, f32[145,16,1]{0,1,2:T(8,128)}, u32[]{:S(2)}, u32[]{:S(2)}) collective-permute-start(f32[145,16,1]{0,1,2:T(8,128)S(1)} %copy.26), channel_id=1, source_target_pairs={{1,0},{2,1},{3,2},{0,3},{5,4},{6,5},{7,6},{4,7},{9,8},{10,9},{11,1... | collective-permute-start | bytes 27848 | tf_op jit(solution)/shard_map/ppermute | solution.py:24
  15.4 0.9 %copy-start.8 = (f32[144]{0:T(256)S(1)}, f32[144]{0:T(256)}, u32[]{:S(2)}) copy-start(f32[144]{0:T(256)} %mul.175) | copy-start | bytes 1732
  16.5 0.7 copy-start.11
  17.2 0.7 copy-start.1
  17.2 0.7 copy-start.3
  20.7 0.7 copy-start.4
  20.7 0.7 copy-start.5
  20.7 0.7 copy-start.6
  23.1 4.1 %copy-start.10 = (f32[1152]{0:T(1024)S(1)}, f32[1152]{0:T(1024)}, u32[]{:S(2)}) copy-start(f32[1152]{0:T(1024)} %param.12) | copy-start | bytes 13828
  23.1 4.4 %copy-start.7 = (s32[2,1152]{1,0:T(2,128)S(1)}, s32[2,1152]{1,0:T(2,128)}, u32[]{:S(2)}) copy-start(s32[2,1152]{1,0:T(2,128)} %param.13) | copy-start | bytes 27652
  23.1 20.9 %all-to-all-start = ((f32[144,16,128]{2,0,1:T(8,128)}), f32[144,16,128]{2,0,1:T(8,128)S(1)}, u32[]{:S(2)}, u32[]{:S(2)}) async-start(f32[144,16,128]{2,0,1:T(8,128)} %copy.31), calls=%async_computation | async-start | bytes 2359296 | tf_op jit(solution)/shard_map/all_to_all | solution.py:116
where the time goes:
time: 79.2 us; the launch traced here: 78.5 us
  other arithmetic  32.7 us (41%)
  local copies, waits for them, and re-layouts  21.1 us (27%)
  waiting for transfers between devices  15.2 us (19%)
  starting transfers between devices  9.15 us (12%)
    scatter-add x2, other arithmetic, spread_rows(): return jax.ops.segment_sum(values, lookup_ids, num_segments=values.shape[0])  17.6 us
    all_to_all x1, waiting for transfers between devices, shards(): lax.all_to_all(turned, 'spec', split_axis=1, concat_axis=0, tiled=True)  15.2 us
    gather x2, local copies, waits for them, and re-layouts, pick_rows(): return jnp.take(values, lookup_ids, axis=0)  6.95 us
    all_to_all x1, starting transfers between devices, shards(): lax.all_to_all(turned, 'spec', split_axis=1, concat_axis=0, tiled=True)  4.07 us
    ppermute x1, starting transfers between devices, extended(): lax.ppermute(tail, axis, [(i, (i + 1) % count) for i in range(count)])  3.02 us
    reshape x1, local copies, waits for them, and re-layouts, shards(): (shifted + dia_coeff * source).reshape(n_comps, point_rows, item_count)  2.75 us
    add x1, other arithmetic, shards(): shifted + dia_coeff * source  2.6 us
    mul x1, other arithmetic, advect_space(): return updated * sea_mask  2.52 us
  transfers between devices with their start and end apart: 3, of which 1 were waited for; matrix products, arithmetic and copies ran while one was open for 7% of the time, Pallas kernels for 0%

commit v1 on v0

v1 whole, which is shorter than its diff:
```python
import functools
import math

import jax
import jax.numpy as jnp
from jax import lax
from jax.experimental import pallas as pl
from jax.experimental.pallas import tpu as pltpu
from jax.sharding import PartitionSpec as P

ND = 36
NF = 32
LANES = 128
WRAP = 3
EDGE = 8
ROWS = 48
PAD = 40

speed_top = 0.6
decline = 0.0953102
dia_coeff = 0.25

MESH = pl.DeviceIdType.MESH
COS = [math.cos(2.0 * math.pi * d / ND) for d in range(ND)]
SIN = [math.sin(2.0 * math.pi * d / ND) for d in range(ND)]


def two_parts(values):
    high = values.astype(jnp.bfloat16)
    low = (values - high.astype(jnp.float32)).astype(jnp.bfloat16)
    return high, low


def picked(values, table, dims):
    high, low = two_parts(values)
    dot = functools.partial(
        lax.dot_general, dimension_numbers=(dims, ((), ())), preferred_element_type=jnp.float32
    )
    return dot(high, table) + dot(low, table)


def one_hot(slots):
    cells = lax.broadcasted_iota(jnp.int32, (2 * LANES, slots.shape[1]), 0)
    return jnp.where(cells == slots, 1.0, 0.0).astype(jnp.bfloat16)


def send_kernel(packed, n_spec, n_tile, grid_rows, n_chan,
                energy, depth, turning, slots, counts, out,
                slot_rows, table, mask, edge, halo, spaced, turned, payload,
                halo_send, halo_recv, send_sem, recv_sem, own_sem):
    me = lax.axis_index("spec")
    tile = lax.axis_index("tile")
    right, left = lax.rem(tile + 1, n_tile), lax.rem(tile + n_tile - 1, n_tile)
    n_freq = n_chan // ND
    cap = slots.shape[2]

    barrier = pltpu.get_barrier_semaphore()

    def greet(step, carry):
        peer = lax.rem(me + step, n_spec)
        pl.semaphore_signal(barrier, inc=1, device_id=(peer, tile), device_id_type=MESH)
        return carry

    lax.fori_loop(1, n_spec, greet, 0)
    for neighbour in (left, right):
        pl.semaphore_signal(barrier, inc=1, device_id=(me, neighbour), device_id_type=MESH)

    slot_rows[...] = jnp.full(slot_rows.shape, -1, jnp.int32)
    slot_rows[:, :, 0:cap] = slots[...]
    rank = lax.broadcasted_iota(jnp.int32, (1, 2 * LANES), 1)
    ones = jnp.ones((8, 2 * LANES), jnp.bfloat16)

    def make_table(block, carry):
        live = jnp.where(rank < counts[block, 0], slot_rows[block], -1)
        spots = one_hot(live)
        table[block, :, 0 : 2 * LANES] = spots
        if packed:
            second = jnp.broadcast_to(live[:, LANES:], (8, LANES))
            second = pltpu.roll(second, LANES // 2, 1)[0:1]
            table[block, :, 2 * LANES :] = one_hot(second)
        sea = lax.dot_general(ones, spots, (((1,), (1,)), ((), ())),
                              preferred_element_type=jnp.float32)
        mask[pl.ds(2 * block, 1), :] = sea[0:1, :LANES]
        mask[pl.ds(2 * block + 1, 1), :] = sea[0:1, LANES:]
        return carry

    lax.fori_loop(0, n_spec, make_table, 0)

    weight = depth[...] * mask[...]
    lane = lax.broadcasted_iota(jnp.int32, (grid_rows, LANES), 1)
    row = lax.broadcasted_iota(jnp.int32, (grid_rows, LANES), 0)

    def scaled(freq):
        number = (me * n_freq + freq).astype(jnp.float32)
        return weight * (speed_top * jnp.exp(jnp.full((grid_rows, LANES), -decline * number)))

    def cell_rows(freq, direction):
        start = pl.multiple_of((freq * ND + direction) * grid_rows, 8)
        return pl.ds(start, grid_rows)

    def make_edge(freq, carry):
        rate = scaled(freq)
        held = jnp.zeros((grid_rows, LANES), jnp.float32)
        for d in range(ND):
            flow = energy[cell_rows(freq, d), :] * rate
            moved = pltpu.roll(flow, (d + 1) % LANES if COS[d] > 0 else d, 1) if d or COS[d] > 0 else flow
            held = jnp.where(lane == d, moved, held)
        edge[freq] = held
        return carry

    lax.fori_loop(0, n_freq, make_edge, 0)
    pl.semaphore_wait(barrier, n_spec + 1)
    copies = []
    for place, neighbour in enumerate((right, left)):
        copy = pltpu.make_async_remote_copy(
            src_ref=edge, dst_ref=halo.at[place], send_sem=halo_send.at[place],
            recv_sem=halo_recv.at[place], device_id=(me, neighbour), device_id_type=MESH)
        copy.start()
        copies.append(copy)

    def advect(freq, carry):
        rate = scaled(freq)
        for d in range(ND):
            value = energy[cell_rows(freq, d), :]
            flow = value * rate
            east, north = abs(COS[d]), abs(SIN[d])
            if COS[d] > 0:
                side = jnp.where(lane == 0, 0.0, pltpu.roll(flow, 1, 1))
            else:
                side = jnp.where(lane == LANES - 1, 0.0, pltpu.roll(flow, LANES - 1, 1))
            total = value - (east + north) * flow + east * side
            if SIN[d] > 0:
                total = total + north * jnp.where(row == 0, 0.0, pltpu.roll(flow, 1, 0))
            elif SIN[d] < 0:
                total = total + north * jnp.where(
                    row == grid_rows - 1, 0.0, pltpu.roll(flow, grid_rows - 1, 0))
            spaced[cell_rows(freq, d), :] = total
        return carry

    lax.fori_loop(0, n_freq, advect, 0)
    for copy in copies:
        copy.wait()

    turn = turning[...]
    stay, ahead, back = 1.0 - jnp.abs(turn), jnp.maximum(turn, 0.0), jnp.maximum(-turn, 0.0)

    def turn_all(freq, carry):
        def whole(d):
            value = spaced[cell_rows(freq, d), :]
            if COS[d] > 0:
                held = halo[0, freq]
                moved = pltpu.roll(held, (LANES - d) % LANES, 1) if d else held
                return value + jnp.where(lane == 0, COS[d] * moved, 0.0)
            held = halo[1, freq]
            moved = pltpu.roll(held, LANES - 1 - d, 1)
            return value + jnp.where(lane == LANES - 1, -COS[d] * moved, 0.0)

        first = whole(0)
        before, here = whole(ND - 1), first
        for d in range(ND):
            after = whole(d + 1) if d + 1 < ND else first
            turned[cell_rows(freq, d), :] = stay * here + ahead * before + back * after
            before, here = here, after
        return carry

    lax.fori_loop(0, n_freq, turn_all, 0)

    def fill(block):
        part = n_chan // 2
        values = jnp.concatenate(
            [turned[pl.ds(2 * block + r, n_chan, stride=grid_rows), :] for r in range(2)], axis=1)
        if packed:
            upper = picked(values[:part], table[block, :, 0 : 2 * LANES], ((1,), (0,)))
            spots = jnp.concatenate(
                [table[block, :, :LANES], table[block, :, 2 * LANES :]], axis=1)
            lower = picked(values[part:], spots, ((1,), (0,)))
            payload[block, 0:part, :] = upper[:, :LANES]
            payload[block, part:n_chan, :] = lower[:, :LANES]
            payload[block, n_chan:, :] = upper[:, LANES:] + lower[:, LANES:]
        else:
            both = picked(values, table[block], ((1,), (0,)))
            payload[block, 0:n_chan, :] = both[:, :LANES]
            payload[block, n_chan:, :] = both[:, LANES:]

    def sending(step):
        peer = lax.rem(me + step, n_spec)
        return peer, pltpu.make_async_remote_copy(
            src_ref=payload.at[peer], dst_ref=out.at[me], send_sem=send_sem.at[step],
            recv_sem=recv_sem.at[step], device_id=(peer, tile), device_id_type=MESH)

    def send(step, carry):
        peer, copy = sending(step)
        fill(peer)
        copy.start()
        return carry

    lax.fori_loop(1, n_spec, send, 0)
    fill(me)
    own = pltpu.make_async_copy(payload.at[me], out.at[me], own_sem)
    own.start()
    own.wait()

    def finish(step, carry):
        _, copy = sending(step)
        copy.wait()
        return carry

    lax.fori_loop(1, n_spec, finish, 0)


def settle_kernel(packed, n_spec, n_chan, points, drift, partners, slots, counts, out,
                  slot_rows, rates, flat, wide, added, fresh):
    me = lax.axis_index("spec")
    total = ND * NF
    cap = slots.shape[2]
    part = n_chan // 2

    eye = (lax.broadcasted_iota(jnp.int32, (LANES, LANES), 0)
           == lax.broadcasted_iota(jnp.int32, (LANES, LANES), 1))
    ones = jnp.ones((LANES, LANES), jnp.float32)
    rates[0:PAD, :] = jnp.zeros((PAD, LANES), jnp.float32)
    rates[PAD + total :, :] = jnp.zeros((PAD, LANES), jnp.float32)
    for chunk in range(total // LANES):
        line = drift[:, chunk * LANES : (chunk + 1) * LANES]
        rates[PAD + chunk * LANES : PAD + (chunk + 1) * LANES, :] = lax.dot_general(
            jnp.where(eye, line, 0.0), ones, (((1,), (0,)), ((), ())),
            precision=lax.Precision.HIGHEST, preferred_element_type=jnp.float32)

    for half in range(2):
        flat[half, 0:PAD, :] = jnp.zeros((PAD, LANES), jnp.float32)
        flat[half, PAD + total :, :] = jnp.zeros((PAD, LANES), jnp.float32)
    for s in range(n_spec):
        at = PAD + s * n_chan
        flat[0, at : at + n_chan, :] = points[s, 0:n_chan, :]
        if packed:
            rest = points[s, n_chan:, :]
            flat[1, at : at + part, :] = rest
            flat[1, at + part : at + n_chan, :] = pltpu.roll(rest, LANES // 2, 1)
        else:
            flat[1, at : at + n_chan, :] = points[s, n_chan:, :]

    def shift(freq, carry):
        here = pl.ds(PAD + freq * ND, ND)
        below = pl.ds(PAD + freq * ND - ND, ND)
        above = pl.ds(PAD + freq * ND + ND, ND)
        stay = 1.0 - jnp.abs(rates[here, :])
        rise = jnp.maximum(rates[below, :], 0.0)
        fall = jnp.maximum(-rates[above, :], 0.0)
        for half in range(2):
            moved = (stay * flat[half, here, :] + rise * flat[half, below, :]
                     + fall * flat[half, above, :])
            wide[half, freq, EDGE : EDGE + ND, :] = moved
            wide[half, freq, EDGE - WRAP : EDGE, :] = moved[ND - WRAP :]
            wide[half, freq, EDGE + ND : EDGE + ND + WRAP, :] = moved[:WRAP]
            added[half, freq] = jnp.zeros((ROWS, LANES), jnp.float32)
        return carry

    lax.fori_loop(0, NF, shift, 0)

    def interact(freq, carry):
        plus, minus = partners[0, freq * ND], partners[1, freq * ND]
        upper, lower = plus // ND, minus // ND
        up = pl.ds(EDGE + plus - upper * ND, ND)
        down = pl.ds(EDGE + minus - lower * ND - ND, ND)
        here = pl.ds(EDGE, ND)
        for half in range(2):
            value = wide[half, freq, here, :]
            p, m = wide[half, upper, up, :], wide[half, lower, down, :]
            quartet = value * (value * (p + m) - 2.0 * (p * m))
            added[half, upper, up, :] = added[half, upper, up, :] + quartet
            added[half, lower, down, :] = added[half, lower, down, :] + quartet
            added[half, freq, here, :] = added[half, freq, here, :] - 2.0 * quartet
        return carry

    lax.fori_loop(0, NF, interact, 0)

    def settle(freq, carry):
        for half in range(2):
            low = added[half, freq, EDGE + ND : EDGE + ND + WRAP, :]
            high = added[half, freq, EDGE - WRAP : EDGE, :]
            added[half, freq, EDGE : EDGE + WRAP, :] += low
            added[half, freq, EDGE + ND - WRAP : EDGE + ND, :] += high
            fresh[half, pl.ds(freq * ND, ND), :] = (
                wide[half, freq, EDGE : EDGE + ND, :]
                + dia_coeff * added[half, freq, EDGE : EDGE + ND, :])
        return carry

    lax.fori_loop(0, NF, settle, 0)

    slot_rows[...] = jnp.full(slot_rows.shape, -1, jnp.int32)
    slot_rows[:, 0:cap] = slots[me]
    rank = lax.broadcasted_iota(jnp.int32, (1, 2 * LANES), 1)
    spots = one_hot(jnp.where(rank < counts[me, 0], slot_rows[...], -1))

    def expand(chunk, carry):
        rows = pl.ds(pl.multiple_of(chunk * LANES, LANES), LANES)
        values = jnp.concatenate([fresh[0, rows, :], fresh[1, rows, :]], axis=1)
        cells = picked(values, spots, ((1,), (1,)))
        for r in range(2):
            out[pl.ds(chunk * 2 * LANES + r, LANES, stride=2), :] = (
                cells[:, r * LANES : (r + 1) * LANES])
        return carry

    lax.fori_loop(0, total // LANES, expand, 0)


def shards(spectrum, depth_speed, turning, drift, partners, sea_slots, sea_counts):
    n_chan, grid_rows, grid_cols = spectrum.shape
    n_spec, n_tile = lax.axis_size("spec"), lax.axis_size("tile")
    cap = sea_slots.shape[2]
    packed = n_chan % 16 == 0 and cap <= 3 * LANES // 2
    load = n_chan * 3 // 2 if packed else n_chan * 2
    total = ND * NF
    f32 = jnp.float32
    vmem = pl.BlockSpec(memory_space=pltpu.VMEM)
    smem = pl.BlockSpec(memory_space=pltpu.SMEM)
    points = pl.pallas_call(
        functools.partial(send_kernel, packed, n_spec, n_tile, grid_rows, n_chan),
        out_shape=jax.ShapeDtypeStruct((n_spec, load, LANES), f32),
        in_specs=[vmem, vmem, vmem, vmem, smem],
        out_specs=pl.BlockSpec(memory_space=pl.ANY),
        scratch_shapes=[
            pltpu.VMEM((n_spec, 1, 2 * LANES), jnp.int32),
            pltpu.VMEM((n_spec, 2 * LANES, (3 if packed else 2) * LANES), jnp.bfloat16),
            pltpu.VMEM((grid_rows, LANES), f32),
            pltpu.VMEM((n_chan // ND, grid_rows, LANES), f32),
            pltpu.VMEM((2, n_chan // ND, grid_rows, LANES), f32),
            pltpu.VMEM((n_chan * grid_rows, LANES), f32),
            pltpu.VMEM((n_chan * grid_rows, LANES), f32),
            pltpu.VMEM((n_spec, load, LANES), f32),
            pltpu.SemaphoreType.DMA((2,)),
            pltpu.SemaphoreType.DMA((2,)),
            pltpu.SemaphoreType.DMA((n_spec,)),
            pltpu.SemaphoreType.DMA((n_spec,)),
            pltpu.SemaphoreType.DMA,
        ],
        compiler_params=pltpu.CompilerParams(
            collective_id=0, has_side_effects=True, vmem_limit_bytes=40 * 2**20),
    )(spectrum.reshape(n_chan * grid_rows, grid_cols), depth_speed, turning, sea_slots, sea_counts)
    settled = pl.pallas_call(
        functools.partial(settle_kernel, packed, n_spec, n_chan),
        out_shape=jax.ShapeDtypeStruct((total * 2, LANES), f32),
        in_specs=[vmem, vmem, smem, vmem, smem],
        out_specs=vmem,
        scratch_shapes=[
            pltpu.VMEM((1, 2 * LANES), jnp.int32),
            pltpu.VMEM((total + 2 * PAD, LANES), f32),
            pltpu.VMEM((2, total + 2 * PAD, LANES), f32),
            pltpu.VMEM((2, NF, ROWS, LANES), f32),
            pltpu.VMEM((2, NF, ROWS, LANES), f32),
            pltpu.VMEM((2, total, LANES), f32),
        ],
        compiler_params=pltpu.CompilerParams(vmem_limit_bytes=40 * 2**20),
    )(points, drift.reshape(1, total), partners, sea_slots, sea_counts)
    return settled.reshape(total, 2, LANES)


def solution(mesh):
    return jax.shard_map(
        shards,
        mesh=mesh,
        in_specs=(
            P("spec", None, "tile"),
            P(None, "tile"),
            P(None, "tile"),
            P(),
            P(),
            P(None, "tile", None),
            P(None, "tile"),
        ),
        out_specs=P(None, "spec", "tile"),
        check_vma=False,
    )
```

time: 79.2 us -> 33.9 us (0.43)
  the two profiles are of different devices: /device:TPU:0 before, /device:TPU:1 now
where the time goes in v1:
time: 33.9 us; the launch traced here: 33.5 us
  Pallas kernels  28.7 us (85%)
  local copies, waits for them, and re-layouts  4.81 us (14%)
    pallas_call x1, Pallas kernels, shards(): pl.pallas_call(functools.partial(send_kernel, packed, n_spec, n_tile, gri...  21.7 us
    pallas_call x1, Pallas kernels, shards(): pl.pallas_call(functools.partial(settle_kernel, packed, n_spec, n_chan),...  7.04 us
    unnamed x11, local copies, waits for them, and re-layouts  4.11 us
    reshape x1, local copies, waits for them, and re-layouts, shards(): drift.reshape(1, total)  0.7 us

profile of v1, /device:TPU:1, one launch (start us, length us, event | category | flops | bytes accessed | tf_op | source)
XLA Modules:
  0.0 33.5 jit_solution(9416049605695208174)
XLA Ops:
  0.0 0.0 copy-start.2
  0.0 0.7 %copy.8.counts = s32[8,1]{1,0:T(8,128)S(1)} copy(s32[8,1]{0,1:T(1,128)} %param.13) | data formatting | bytes 64 | tf_op args[6]
  0.7 0.7 %reshape.10.drift = f32[1,1152]{1,0:T(1,128)S(1)} reshape(f32[1152]{0:T(1024)} %param.10) | data formatting | bytes 9216 | tf_op jit(solution)/shard_map/reshape | solution.py:354
  1.4 0.0 copy-start
  1.4 1.3 %copy-done = f32[144,16,128]{2,1,0:T(8,128)S(1)} copy-done((f32[144,16,128]{2,1,0:T(8,128)S(1)}, f32[144,16,128]{2,1,0:T(8,128)}, u32[]{:S(2)}) %copy-start) | copy-done | bytes 1179672
  2.7 0.0 copy-start.1
  2.7 0.7 %copy-done.1 = s32[8,1,192]{2,1,0:T(1,128)S(1)} copy-done((s32[8,1,192]{2,1,0:T(1,128)S(1)}, s32[8,1,192]{2,1,0:T(1,128)}, u32[]{:S(2)}) %copy-start.1) | copy-done | bytes 6168
  3.4 0.0 copy-start.3
  3.4 0.7 %copy-done.3 = f32[16,128]{1,0:T(8,128)S(1)} copy-done((f32[16,128]{1,0:T(8,128)S(1)}, f32[16,128]{1,0:T(8,128)}, u32[]{:S(2)}) %copy-start.3) | copy-done | bytes 8216
  4.1 0.0 copy-start.4
  4.1 0.7 %copy-done.4 = f32[16,128]{1,0:T(8,128)S(1)} copy-done((f32[16,128]{1,0:T(8,128)S(1)}, f32[16,128]{1,0:T(8,128)}, u32[]{:S(2)}) %copy-start.4) | copy-done | bytes 8216
  4.8 21.7 %shard_map.73.points = f32[8,216,128]{2,1,0:T(8,128)S(1)} custom-call(f32[2304,128]{1,0:T(8,128)S(1)} %bitcast.2, f32[16,128]{1,0:T(8,128)S(1)} %copy-done.3, f32[16,128]{1,0:T(8,128)S(1)} %copy-done.4, s32[8,1,192]{2,1,0:T(1,128)S(1)} %copy-done.1, s32[8,1]{1,0:T(8,128)S(1)} %copy.8.counts), custom_call_target="tpu_custom_call" | custom-call | tf_op jit(solution)/shard_map/pallas_call | solution.py:317
  26.5 0.0 copy-done.2
  26.5 7.0 %shard_map.74 = f32[2304,128]{1,0:T(8,128)} custom-call(f32[8,216,128]{2,1,0:T(8,128)S(1)} %shard_map.73.points, f32[1,1152]{1,0:T(1,128)S(1)} %reshape.10.drift, s32[2,1152]{1,0:T(2,128)S(1)} %copy-done.2, s32[8,1,192]{2,1,0:T(1,128)S(1)} %copy-done.1, s32[8,1]{1,0:T(8,128)S(1)} %copy.8.counts), custom_call_target="tpu_custom_call" | custom-call | tf_op jit(solution)/shard_map/pallas_call | solution.py:340
Async XLA Ops:
  0.0 26.5 %copy-start.2 = (s32[2,1152]{1,0:T(2,128)S(1)}, s32[2,1152]{1,0:T(2,128)}, u32[]{:S(2)}) copy-start(s32[2,1152]{1,0:T(2,128)} %partners.1) | copy-start | bytes 27652
  1.4 1.3 %copy-start = (f32[144,16,128]{2,1,0:T(8,128)S(1)}, f32[144,16,128]{2,1,0:T(8,128)}, u32[]{:S(2)}) copy-start(f32[144,16,128]{2,1,0:T(8,128)} %param.7) | copy-start | bytes 3538948
  2.7 0.7 %copy-start.1 = (s32[8,1,192]{2,1,0:T(1,128)S(1)}, s32[8,1,192]{2,1,0:T(1,128)}, u32[]{:S(2)}) copy-start(s32[8,1,192]{2,1,0:T(1,128)} %slots.3) | copy-start | bytes 18436
  3.4 0.7 %copy-start.3 = (f32[16,128]{1,0:T(8,128)S(1)}, f32[16,128]{1,0:T(8,128)}, u32[]{:S(2)}) copy-start(f32[16,128]{1,0:T(8,128)} %depth.1) | copy-start | bytes 24580
  4.1 0.7 %copy-start.4 = (f32[16,128]{1,0:T(8,128)S(1)}, f32[16,128]{1,0:T(8,128)}, u32[]{:S(2)}) copy-start(f32[16,128]{1,0:T(8,128)} %turning.1) | copy-start | bytes 24580

commit v2 on v1

v2 whole, which is shorter than its diff:
```python
import functools
import math

import jax
import jax.numpy as jnp
from jax import lax
from jax.experimental import pallas as pl
from jax.experimental.pallas import tpu as pltpu
from jax.sharding import PartitionSpec as P

ND = 36
NF = 32
LANES = 128
WRAP = 3
EDGE = 8
ROWS = 48
PAD = 40
PARTS = 3
VMEM_ALL = 64 * 2**20

speed_top = 0.6
decline = 0.0953102
dia_coeff = 0.25

MESH = pl.DeviceIdType.MESH
COS = [math.cos(2.0 * math.pi * d / ND) for d in range(ND)]
SIN = [math.sin(2.0 * math.pi * d / ND) for d in range(ND)]


def two_parts(values):
    high = values.astype(jnp.bfloat16)
    low = (values - high.astype(jnp.float32)).astype(jnp.bfloat16)
    return high, low


def picked(values, table, dims):
    high, low = two_parts(values)
    dot = functools.partial(
        lax.dot_general, dimension_numbers=(dims, ((), ())), preferred_element_type=jnp.float32
    )
    return dot(high, table) + dot(low, table)


def one_hot(slots):
    cells = lax.broadcasted_iota(jnp.int32, (2 * LANES, slots.shape[1]), 0)
    return jnp.where(cells == slots, 1.0, 0.0).astype(jnp.bfloat16)


def step_kernel(packed, n_spec, n_tile, grid_rows, n_chan,
                spectrum_in, depth_in, turning_in, drift_in, partners_in, slots_in, counts_in,
                fresh_out, spots_out,
                energy, depth, turning, drift, partners, slots, counts, in_sem,
                slot_rows, table, mask, edge, halo, spaced, turned,
                first, second, first_in, second_in,
                rates, coef, flat, wide, quartets, route, fresh, out_sem,
                halo_send, halo_recv, send_sem, recv_sem):
    me = lax.axis_index("spec")
    tile = lax.axis_index("tile")
    right, left = lax.rem(tile + 1, n_tile), lax.rem(tile + n_tile - 1, n_tile)
    n_freq = n_chan // ND
    total = ND * NF
    cap = slots.shape[2]
    part = n_chan // 2

    pairs = ((slots_in, slots), (counts_in, counts), (depth_in, depth), (spectrum_in, energy),
             (turning_in, turning), (drift_in, drift), (partners_in, partners))
    loads = [pltpu.make_async_copy(a, b, in_sem.at[i]) for i, (a, b) in enumerate(pairs)]
    for load in loads:
        load.start()

    barrier = pltpu.get_barrier_semaphore()

    def greet(step, carry):
        peer = lax.rem(me + step, n_spec)
        pl.semaphore_signal(barrier, inc=1, device_id=(peer, tile), device_id_type=MESH)
        return carry

    lax.fori_loop(1, n_spec, greet, 0)
    for neighbour in (left, right):
        pl.semaphore_signal(barrier, inc=1, device_id=(me, neighbour), device_id_type=MESH)

    slot_rows[...] = jnp.full(slot_rows.shape, -1, jnp.int32)
    loads[0].wait()
    loads[1].wait()
    slot_rows[:, :, 0:cap] = slots[...]
    rank = lax.broadcasted_iota(jnp.int32, (1, 2 * LANES), 1)
    ones = jnp.ones((8, 2 * LANES), jnp.bfloat16)

    def make_table(block, carry):
        live = jnp.where(rank < counts[0, block], slot_rows[block], -1)
        spots = one_hot(live)
        table[block, :, 0 : 2 * LANES] = spots
        if packed:
            rolled = jnp.broadcast_to(live[:, LANES:], (8, LANES))
            rolled = pltpu.roll(rolled, LANES // 2, 1)[0:1]
            table[block, :, 2 * LANES :] = one_hot(rolled)
        sea = lax.dot_general(ones, spots, (((1,), (1,)), ((), ())),
                              preferred_element_type=jnp.float32)
        mask[pl.ds(2 * block, 1), :] = sea[0:1, :LANES]
        mask[pl.ds(2 * block + 1, 1), :] = sea[0:1, LANES:]
        return carry

    lax.fori_loop(0, n_spec, make_table, 0)

    loads[2].wait()
    loads[3].wait()
    weight = depth[...] * mask[...]
    lane = lax.broadcasted_iota(jnp.int32, (grid_rows, LANES), 1)
    row = lax.broadcasted_iota(jnp.int32, (grid_rows, LANES), 0)

    def scaled(freq):
        number = (me * n_freq + freq).astype(jnp.float32)
        return weight * (speed_top * jnp.exp(jnp.full((grid_rows, LANES), -decline * number)))

    def cell_rows(freq, direction):
        start = pl.multiple_of((freq * ND + direction) * grid_rows, 8)
        return pl.ds(start, grid_rows)

    def make_edge(freq, carry):
        rate = scaled(freq)
        held = jnp.zeros((grid_rows, LANES), jnp.float32)
        for d in range(ND):
            flow = energy[cell_rows(freq, d), :] * rate
            moved = pltpu.roll(flow, d + 1 if COS[d] > 0 else d, 1)
            held = jnp.where(lane == d, moved, held)
        edge[freq] = held
        return carry

    lax.fori_loop(0, n_freq, make_edge, 0)
    pl.semaphore_wait(barrier, n_spec + 1)
    copies = []
    for place, neighbour in enumerate((right, left)):
        copy = pltpu.make_async_remote_copy(
            src_ref=edge, dst_ref=halo.at[place], send_sem=halo_send.at[place],
            recv_sem=halo_recv.at[place], device_id=(me, neighbour), device_id_type=MESH)
        copy.start()
        copies.append(copy)

    def advect(freq, carry):
        rate = scaled(freq)
        for d in range(ND):
            value = energy[cell_rows(freq, d), :]
            flow = value * rate
            east, north = abs(COS[d]), abs(SIN[d])
            if COS[d] > 0:
                side = jnp.where(lane == 0, 0.0, pltpu.roll(flow, 1, 1))
            else:
                side = jnp.where(lane == LANES - 1, 0.0, pltpu.roll(flow, LANES - 1, 1))
            result = value - (east + north) * flow + east * side
            if SIN[d] > 0:
                result = result + north * jnp.where(row == 0, 0.0, pltpu.roll(flow, 1, 0))
            elif SIN[d] < 0:
                result = result + north * jnp.where(
                    row == grid_rows - 1, 0.0, pltpu.roll(flow, grid_rows - 1, 0))
            spaced[cell_rows(freq, d), :] = result
        return carry

    def turn_all(freq, carry):
        turn = turning[...]
        stay, ahead = 1.0 - jnp.abs(turn), jnp.maximum(turn, 0.0)
        back = jnp.maximum(-turn, 0.0)

        def whole(d):
            value = spaced[cell_rows(freq, d), :]
            if COS[d] > 0:
                held = halo[0, freq]
                moved = pltpu.roll(held, (LANES - d) % LANES, 1) if d else held
                return value + jnp.where(lane == 0, COS[d] * moved, 0.0)
            held = halo[1, freq]
            moved = pltpu.roll(held, LANES - 1 - d, 1)
            return value + jnp.where(lane == LANES - 1, -COS[d] * moved, 0.0)

        start = whole(0)
        before, here = whole(ND - 1), start
        for d in range(ND):
            after = whole(d + 1) if d + 1 < ND else start
            turned[cell_rows(freq, d), :] = stay * here + ahead * before + back * after
            before, here = here, after
        return carry

    def cells_of(block, low, count):
        return jnp.concatenate(
            [turned[pl.ds(low * grid_rows + 2 * block + r, count, stride=grid_rows), :]
             for r in range(2)], axis=1)

    def sending(kind, step):
        peer = lax.rem(me + step, n_spec)
        if kind == 2:
            src, dst = second.at[peer], second_in.at[me]
        elif packed:
            rows = pl.ds(kind * part, part)
            src, dst = first.at[peer, rows], first_in.at[me, rows]
        else:
            src, dst = first.at[peer], first_in.at[me]
        return pltpu.make_async_remote_copy(
            src_ref=src, dst_ref=dst, send_sem=send_sem.at[kind, step],
            recv_sem=recv_sem.at[kind, step], device_id=(peer, tile), device_id_type=MESH)

    def fill_upper(block):
        both = picked(cells_of(block, 0, part), table[block, :, 0 : 2 * LANES], ((1,), (0,)))
        first[block, 0:part, :] = both[:, :LANES]
        second[block] = both[:, LANES:]

    def fill_lower(block):
        spots = jnp.concatenate([table[block, :, :LANES], table[block, :, 2 * LANES :]], axis=1)
        both = picked(cells_of(block, part, part), spots, ((1,), (0,)))
        first[block, part:, :] = both[:, :LANES]
        second[block] = second[block] + both[:, LANES:]

    def fill_whole(block):
        both = picked(cells_of(block, 0, n_chan), table[block], ((1,), (0,)))
        first[block] = both[:, :LANES]
        second[block] = both[:, LANES:]

    def stage(fill, kind):
        def body(step, carry):
            fill(lax.rem(me + step, n_spec))
            sending(kind, step).start()
            return carry

        lax.fori_loop(1, n_spec, body, 0)

    def start_second(step, carry):
        sending(2, step).start()
        return carry

    def arrive():
        for copy in copies:
            copy.wait()
        loads[4].wait()

    if packed and n_freq % 2 == 0:
        half = n_freq // 2
        lax.fori_loop(0, half, advect, 0)
        arrive()
        lax.fori_loop(0, half, turn_all, 0)
        stage(fill_upper, 0)
        lax.fori_loop(half, n_freq, advect, 0)
        lax.fori_loop(half, n_freq, turn_all, 0)
        stage(fill_lower, 1)
        lax.fori_loop(1, n_spec, start_second, 0)
        fill_upper(me)
        fill_lower(me)
        kinds = (0, 1)
    else:
        lax.fori_loop(0, n_freq, advect, 0)
        arrive()
        lax.fori_loop(0, n_freq, turn_all, 0)
        stage(fill_whole, 0)
        lax.fori_loop(1, n_spec, start_second, 0)
        fill_whole(me)
        kinds = (0,)

    saves = [pltpu.make_async_copy(table.at[me, :, 0 : 2 * LANES], spots_out, out_sem.at[2])]
    saves[0].start()
    loads[5].wait()
    loads[6].wait()
    eye = (lax.broadcasted_iota(jnp.int32, (LANES, LANES), 0)
           == lax.broadcasted_iota(jnp.int32, (LANES, LANES), 1))
    square = jnp.ones((LANES, LANES), jnp.float32)
    rates[0:PAD, :] = jnp.zeros((PAD, LANES), jnp.float32)
    rates[PAD + total :, :] = jnp.zeros((PAD, LANES), jnp.float32)
    for chunk in range(total // LANES):
        line = drift[pl.ds(chunk * LANES, LANES)].reshape(1, LANES)
        rates[PAD + chunk * LANES : PAD + (chunk + 1) * LANES, :] = lax.dot_general(
            jnp.where(eye, line, 0.0), square, (((1,), (0,)), ((), ())),
            precision=lax.Precision.HIGHEST, preferred_element_type=jnp.float32)

    def prepare(freq, carry):
        at = PAD + freq * ND
        coef[0, freq, 0:ND, :] = 1.0 - jnp.abs(rates[pl.ds(at, ND), :])
        coef[1, freq, 0:ND, :] = jnp.maximum(rates[pl.ds(at - ND, ND), :], 0.0)
        coef[2, freq, 0:ND, :] = jnp.maximum(-rates[pl.ds(at + ND, ND), :], 0.0)
        plus, minus = partners[0, freq * ND], partners[1, freq * ND]
        route[0, freq] = plus // ND
        route[1, freq] = plus - (plus // ND) * ND
        route[2, freq] = minus // ND
        route[3, freq] = lax.rem(ND - (minus - (minus // ND) * ND), ND)
        return carry

    lax.fori_loop(0, NF, prepare, 0)
    quartets[NF] = jnp.zeros((ROWS, LANES), jnp.float32)
    flat[0:PAD, :] = jnp.zeros((PAD, LANES), jnp.float32)
    flat[PAD + total :, :] = jnp.zeros((PAD, LANES), jnp.float32)

    def spread(place, freq, values):
        place[freq, EDGE : EDGE + ND, :] = values
        place[freq, EDGE - WRAP : EDGE, :] = values[ND - WRAP :]
        place[freq, EDGE + ND : EDGE + ND + WRAP, :] = values[:WRAP]

    here = pl.ds(EDGE, ND)

    def settle(half):
        def shift(freq, carry):
            at = PAD + freq * ND
            spread(wide, freq, coef[0, freq, 0:ND, :] * flat[pl.ds(at, ND), :]
                   + coef[1, freq, 0:ND, :] * flat[pl.ds(at - ND, ND), :]
                   + coef[2, freq, 0:ND, :] * flat[pl.ds(at + ND, ND), :])
            return carry

        def interact(freq, carry):
            value = wide[freq, here, :]
            p = wide[route[0, freq], pl.ds(EDGE + route[1, freq], ND), :]
            m = wide[route[2, freq], pl.ds(EDGE - route[3, freq], ND), :]
            spread(quartets, freq, value * (value * (p + m) - 2.0 * (p * m)))
            return carry

        def gather(freq, carry):
            source = -2.0 * quartets[freq, here, :]
            for off in (1, 2, 3):
                f = jnp.maximum(freq - off, 0)
                found = (route[0, f] == freq) & (freq >= off)
                block = jnp.where(found, f, NF)
                source = source + quartets[block, pl.ds(EDGE - route[1, f], ND), :]
                f = jnp.minimum(freq + off, NF - 1)
                found = (route[2, f] == freq) & (freq + off < NF)
                block = jnp.where(found, f, NF)
                source = source + quartets[block, pl.ds(EDGE + route[3, f], ND), :]
            fresh[half, pl.ds(freq * ND, ND), :] = wide[freq, here, :] + dia_coeff * source
            return carry

        lax.fori_loop(0, NF, shift, 0)
        lax.fori_loop(0, NF, interact, 0)
        lax.fori_loop(0, NF, gather, 0)
        last = pl.ds((NF - 1) * ND, ND)
        fresh[half, last, :] = fresh[half, last, :] + dia_coeff * (
            quartets[NF - 1, pl.ds(EDGE - route[1, NF - 1], ND), :])
        fresh[half, 0:ND, :] = fresh[half, 0:ND, :] + dia_coeff * (
            quartets[0, pl.ds(EDGE + route[3, 0], ND), :])
        save = pltpu.make_async_copy(fresh.at[half], fresh_out.at[half], out_sem.at[half])
        save.start()
        saves.append(save)

    def unpack_first(source, cells):
        flat[pl.ds(PAD + source * n_chan, n_chan), :] = cells

    def unpack_second(source, cells):
        at = PAD + source * n_chan
        if packed:
            flat[pl.ds(at, part), :] = cells
            flat[pl.ds(at + part, part), :] = pltpu.roll(cells, LANES // 2, 1)
        else:
            flat[pl.ds(at, n_chan), :] = cells

    def take_first(step, carry):
        source = lax.rem(me + n_spec - step, n_spec)
        for kind in kinds:
            sending(kind, step).wait_recv()
        unpack_first(source, first_in[source])
        return carry

    def take_second(step, carry):
        source = lax.rem(me + n_spec - step, n_spec)
        sending(2, step).wait_recv()
        unpack_second(source, second_in[source])
        return carry

    unpack_first(me, first[me])
    lax.fori_loop(1, n_spec, take_first, 0)
    settle(0)
    unpack_second(me, second[me])
    lax.fori_loop(1, n_spec, take_second, 0)
    settle(1)

    def finish(step, carry):
        for kind in kinds + (2,):
            sending(kind, step).wait_send()
        return carry

    lax.fori_loop(1, n_spec, finish, 0)
    for save in saves:
        save.wait()


def expand_kernel(fresh, spots, out):
    def expand(chunk, carry):
        rows = pl.ds(pl.multiple_of(chunk * LANES, LANES), LANES)
        values = jnp.concatenate([fresh[0, rows, :], fresh[1, rows, :]], axis=1)
        cells = picked(values, spots[...], ((1,), (1,)))
        for r in range(2):
            out[pl.ds(chunk * 2 * LANES + r, LANES, stride=2), :] = (
                cells[:, r * LANES : (r + 1) * LANES])
        return carry

    lax.fori_loop(0, fresh.shape[1] // LANES, expand, 0)


def shards(spectrum, depth_speed, turning, drift, partners, sea_slots, sea_counts):
    n_chan, grid_rows, grid_cols = spectrum.shape
    n_spec, n_tile = lax.axis_size("spec"), lax.axis_size("tile")
    cap = sea_slots.shape[2]
    packed = n_chan % 16 == 0 and n_chan // ND % 2 == 0 and cap <= 3 * LANES // 2
    n_freq = n_chan // ND
    rest = n_chan // 2 if packed else n_chan
    total = ND * NF
    f32 = jnp.float32
    hbm = pl.BlockSpec(memory_space=pltpu.HBM)
    fresh, spots = pl.pallas_call(
        functools.partial(step_kernel, packed, n_spec, n_tile, grid_rows, n_chan),
        out_shape=(jax.ShapeDtypeStruct((2, total, LANES), f32),
                   jax.ShapeDtypeStruct((2 * LANES, 2 * LANES), jnp.bfloat16)),
        in_specs=[hbm] * 7,
        out_specs=(hbm, hbm),
        scratch_shapes=[
            pltpu.VMEM((n_chan * grid_rows, LANES), f32),
            pltpu.VMEM((grid_rows, LANES), f32),
            pltpu.VMEM((grid_rows, LANES), f32),
            pltpu.VMEM((total,), f32),
            pltpu.SMEM((2, total), jnp.int32),
            pltpu.VMEM((n_spec, 1, cap), jnp.int32),
            pltpu.SMEM((1, n_spec), jnp.int32),
            pltpu.SemaphoreType.DMA((7,)),
            pltpu.VMEM((n_spec, 1, 2 * LANES), jnp.int32),
            pltpu.VMEM((n_spec, 2 * LANES, (3 if packed else 2) * LANES), jnp.bfloat16),
            pltpu.VMEM((grid_rows, LANES), f32),
            pltpu.VMEM((n_freq, grid_rows, LANES), f32),
            pltpu.VMEM((2, n_freq, grid_rows, LANES), f32),
            pltpu.VMEM((n_chan * grid_rows, LANES), f32),
            pltpu.VMEM((n_chan * grid_rows, LANES), f32),
            pltpu.VMEM((n_spec, n_chan, LANES), f32),
            pltpu.VMEM((n_spec, rest, LANES), f32),
            pltpu.VMEM((n_spec, n_chan, LANES), f32),
            pltpu.VMEM((n_spec, rest, LANES), f32),
            pltpu.VMEM((total + 2 * PAD, LANES), f32),
            pltpu.VMEM((3, NF, PAD, LANES), f32),
            pltpu.VMEM((total + 2 * PAD, LANES), f32),
            pltpu.VMEM((NF, ROWS, LANES), f32),
            pltpu.VMEM((NF + 1, ROWS, LANES), f32),
            pltpu.SMEM((4, NF), jnp.int32),
            pltpu.VMEM((2, total, LANES), f32),
            pltpu.SemaphoreType.DMA((3,)),
            pltpu.SemaphoreType.DMA((2,)),
            pltpu.SemaphoreType.DMA((2,)),
            pltpu.SemaphoreType.DMA((3, n_spec)),
            pltpu.SemaphoreType.DMA((3, n_spec)),
        ],
        compiler_params=pltpu.CompilerParams(
            collective_id=0, has_side_effects=True, vmem_limit_bytes=VMEM_ALL),
    )(spectrum.reshape(n_chan * grid_rows, grid_cols), depth_speed, turning, drift,
      partners, sea_slots, sea_counts.T)
    settled = pl.pallas_call(
        expand_kernel,
        out_shape=jax.ShapeDtypeStruct((total * 2, LANES), f32),
        grid=(PARTS,),
        in_specs=[
            pl.BlockSpec((2, total // PARTS, LANES), lambda i: (0, i, 0)),
            pl.BlockSpec((2 * LANES, 2 * LANES), lambda i: (0, 0)),
        ],
        out_specs=pl.BlockSpec((2 * total // PARTS, LANES), lambda i: (i, 0)),
        compiler_params=pltpu.CompilerParams(vmem_limit_bytes=VMEM_ALL),
    )(fresh, spots)
    return settled.reshape(total, 2, LANES)


def solution(mesh):
    return jax.shard_map(
        shards,
        mesh=mesh,
        in_specs=(
            P("spec", None, "tile"),
            P(None, "tile"),
            P(None, "tile"),
            P(),
            P(),
            P(None, "tile", None),
            P(None, "tile"),
        ),
        out_specs=P(None, "spec", "tile"),
        check_vma=False,
    )
```

time: 33.9 us -> 30.4 us (0.90)
  local copies, waits for them, and re-layouts: 4.81 us -> 0 us
  Pallas kernels: 28.7 us -> 30.2 us
    unnamed x11 -> x0, local copies, waits for them, and re-layouts: 4.11 us -> none
    pallas_call x2, Pallas kernels: 28.7 us -> 30.2 us  [the longest x1 25.9 us: shards(): pl.pallas_call(functools.partial(step_kernel, packed, n_spec, n_tile, gri...]
    reshape x1 -> x0, local copies, waits for them, and re-layouts: 0.7 us -> none  [shards(): drift.reshape(1, total)]
where the time goes in v2:
time: 30.4 us; the launch traced here: 30.2 us
  Pallas kernels  30.2 us (99%)
    pallas_call x1, Pallas kernels, shards(): pl.pallas_call(functools.partial(step_kernel, packed, n_spec, n_tile, gri...  25.9 us
    pallas_call x1, Pallas kernels, shards(): pl.pallas_call(expand_kernel, out_shape=jax.ShapeDtypeStruct((total * 2,...  4.29 us

profile of v2, /device:TPU:1, one launch (start us, length us, event | category | flops | bytes accessed | tf_op | source)
XLA Modules:
  0.0 30.2 jit_solution(6170636281859019440)
XLA Ops:
  0.0 25.9 %shard_map.73 = (f32[2,1152,128]{2,1,0:T(8,128)}, bf16[256,256]{1,0:T(8,128)(2,1)}) custom-call(f32[2304,128]{1,0:T(8,128)} %bitcast.3, f32[16,128]{1,0:T(8,128)} %depth_in.1, f32[16,128]{1,0:T(8,128)} %turning_in.1, f32[1152]{0:T(1024)} %drift_in.1, s32[2,1152]{1,0:T(2,128)} %partners_in.1, s32[8,1,192]{2,1,0:T(1,128)} %slots_in.1, s32[1,8]{1,0:T(1,128)} %bitcast.4), custom_call_target="tpu_custom_call" | custom-call | tf_op jit(solution)/shard_map/pallas_call | solution.py:398
  25.9 4.3 %shard_map.74 = f32[2304,128]{1,0:T(8,128)} custom-call(f32[2,1152,128]{2,1,0:T(8,128)} %get-tuple-element.7.fresh, bf16[256,256]{1,0:T(8,128)(2,1)} %get-tuple-element.8.spots), custom_call_target="tpu_custom_call" | custom-call | tf_op jit(solution)/shard_map/pallas_call | solution.py:441

commit v3 on v2

--- a/solution.py
+++ b/solution.py
@@ -15,7 +15,6 @@
 EDGE = 8
 ROWS = 48
 PAD = 40
-PARTS = 3
 VMEM_ALL = 64 * 2**20
 
 speed_top = 0.6
@@ -48,11 +47,11 @@
 
 def step_kernel(packed, n_spec, n_tile, grid_rows, n_chan,
                 spectrum_in, depth_in, turning_in, drift_in, partners_in, slots_in, counts_in,
-                fresh_out, spots_out,
+                out,
                 energy, depth, turning, drift, partners, slots, counts, in_sem,
                 slot_rows, table, mask, edge, halo, spaced, turned,
                 first, second, first_in, second_in,
-                rates, coef, flat, wide, quartets, route, fresh, out_sem,
+                rates, coef, flat, wide, quartets, route, fresh, whole_out, spots, lists, out_sem,
                 halo_send, halo_recv, send_sem, recv_sem):
     me = lax.axis_index("spec")
     tile = lax.axis_index("tile")
@@ -84,23 +83,22 @@
     loads[1].wait()
     slot_rows[:, :, 0:cap] = slots[...]
     rank = lax.broadcasted_iota(jnp.int32, (1, 2 * LANES), 1)
-    ones = jnp.ones((8, 2 * LANES), jnp.bfloat16)
+    lists[...] = jnp.full(lists.shape, -1.0, jnp.float32)
+    for block in range(n_spec):
+        live = jnp.where(rank < counts[0, block], slot_rows[block], -1)
+        slot_rows[block] = live
+        lists[block : block + 1, :] = live.astype(jnp.float32)
+    columns = jnp.transpose(lists[...])
+    cell = lax.broadcasted_iota(jnp.int32, (2 * LANES, 2 * LANES), 1).astype(jnp.float32)
+    for block in range(n_spec):
+        hits = jnp.where(columns[:, block : block + 1] == cell, 1.0, 0.0)
+        sea = jnp.sum(hits, axis=0, keepdims=True)
+        for r in range(2):
+            mask[2 * block + r : 2 * block + r + 1, :] = sea[:, r * LANES : (r + 1) * LANES]
 
     def make_table(block, carry):
-        live = jnp.where(rank < counts[0, block], slot_rows[block], -1)
-        spots = one_hot(live)
-        table[block, :, 0 : 2 * LANES] = spots
-        if packed:
-            rolled = jnp.broadcast_to(live[:, LANES:], (8, LANES))
-            rolled = pltpu.roll(rolled, LANES // 2, 1)[0:1]
-            table[block, :, 2 * LANES :] = one_hot(rolled)
-        sea = lax.dot_general(ones, spots, (((1,), (1,)), ((), ())),
-                              preferred_element_type=jnp.float32)
-        mask[pl.ds(2 * block, 1), :] = sea[0:1, :LANES]
-        mask[pl.ds(2 * block + 1, 1), :] = sea[0:1, LANES:]
-        return carry
-
-    lax.fori_loop(0, n_spec, make_table, 0)
+        table[block] = one_hot(slot_rows[block])
+        return carry
 
     loads[2].wait()
     loads[3].wait()
@@ -115,6 +113,13 @@
     def cell_rows(freq, direction):
         start = pl.multiple_of((freq * ND + direction) * grid_rows, 8)
         return pl.ds(start, grid_rows)
+
+    def placed(freq, direction):
+        if not packed:
+            return cell_rows(freq, direction)
+        wing = ND // 2
+        at = (freq // 2) * 2 * ND + (direction // wing) * ND + lax.rem(freq, 2) * wing
+        return pl.ds(pl.multiple_of((at + direction % wing) * grid_rows, 8), grid_rows)
 
     def make_edge(freq, carry):
         rate = scaled(freq)
@@ -135,6 +140,7 @@
             recv_sem=halo_recv.at[place], device_id=(me, neighbour), device_id_type=MESH)
         copy.start()
         copies.append(copy)
+    lax.fori_loop(0, n_spec, make_table, 0)
 
     def advect(freq, carry):
         rate = scaled(freq)
@@ -174,7 +180,7 @@
         before, here = whole(ND - 1), start
         for d in range(ND):
             after = whole(d + 1) if d + 1 < ND else start
-            turned[cell_rows(freq, d), :] = stay * here + ahead * before + back * after
+            turned[placed(freq, d), :] = stay * here + ahead * before + back * after
             before, here = here, after
         return carry
 
@@ -183,12 +189,14 @@
             [turned[pl.ds(low * grid_rows + 2 * block + r, count, stride=grid_rows), :]
              for r in range(2)], axis=1)
 
+    last_kind = n_chan // (2 * ND) if packed else 1
+
     def sending(kind, step):
         peer = lax.rem(me + step, n_spec)
-        if kind == 2:
+        if kind == last_kind:
             src, dst = second.at[peer], second_in.at[me]
         elif packed:
-            rows = pl.ds(kind * part, part)
+            rows = pl.ds(kind * 2 * ND, 2 * ND)
             src, dst = first.at[peer, rows], first_in.at[me, rows]
         else:
             src, dst = first.at[peer], first_in.at[me]
@@ -196,16 +204,12 @@
             src_ref=src, dst_ref=dst, send_sem=send_sem.at[kind, step],
             recv_sem=recv_sem.at[kind, step], device_id=(peer, tile), device_id_type=MESH)
 
-    def fill_upper(block):
-        both = picked(cells_of(block, 0, part), table[block, :, 0 : 2 * LANES], ((1,), (0,)))
-        first[block, 0:part, :] = both[:, :LANES]
-        second[block] = both[:, LANES:]
-
-    def fill_lower(block):
-        spots = jnp.concatenate([table[block, :, :LANES], table[block, :, 2 * LANES :]], axis=1)
-        both = picked(cells_of(block, part, part), spots, ((1,), (0,)))
-        first[block, part:, :] = both[:, :LANES]
-        second[block] = second[block] + both[:, LANES:]
+    def fill_pair(pair, block):
+        both = picked(cells_of(block, pair * 2 * ND, 2 * ND), table[block], ((1,), (0,)))
+        first[block, pair * 2 * ND : (pair + 1) * 2 * ND, :] = both[:, :LANES]
+        rest = both[:, LANES:]
+        second[block, pair * ND : (pair + 1) * ND, :] = (
+            rest[:ND] + pltpu.roll(rest, LANES // 2, 1)[ND:])
 
     def fill_whole(block):
         both = picked(cells_of(block, 0, n_chan), table[block], ((1,), (0,)))
@@ -221,7 +225,7 @@
         lax.fori_loop(1, n_spec, body, 0)
 
     def start_second(step, carry):
-        sending(2, step).start()
+        sending(last_kind, step).start()
         return carry
 
     def arrive():
@@ -229,19 +233,16 @@
             copy.wait()
         loads[4].wait()
 
-    if packed and n_freq % 2 == 0:
-        half = n_freq // 2
-        lax.fori_loop(0, half, advect, 0)
-        arrive()
-        lax.fori_loop(0, half, turn_all, 0)
-        stage(fill_upper, 0)
-        lax.fori_loop(half, n_freq, advect, 0)
-        lax.fori_loop(half, n_freq, turn_all, 0)
-        stage(fill_lower, 1)
+    if packed:
+        for pair in range(last_kind):
+            lax.fori_loop(2 * pair, 2 * pair + 2, advect, 0)
+            if pair == 0:
+                arrive()
+            lax.fori_loop(2 * pair, 2 * pair + 2, turn_all, 0)
+            stage(functools.partial(fill_pair, pair), pair)
         lax.fori_loop(1, n_spec, start_second, 0)
-        fill_upper(me)
-        fill_lower(me)
-        kinds = (0, 1)
+        for pair in range(last_kind):
+            fill_pair(pair, me)
     else:
         lax.fori_loop(0, n_freq, advect, 0)
         arrive()
@@ -249,10 +250,9 @@
         stage(fill_whole, 0)
         lax.fori_loop(1, n_spec, start_second, 0)
         fill_whole(me)
-        kinds = (0,)
-
-    saves = [pltpu.make_async_copy(table.at[me, :, 0 : 2 * LANES], spots_out, out_sem.at[2])]
-    saves[0].start()
+    kinds = tuple(range(last_kind))
+
+    spots[...] = jnp.transpose(table[me].astype(jnp.float32)).astype(jnp.bfloat16)
     loads[5].wait()
     loads[6].wait()
     eye = (lax.broadcasted_iota(jnp.int32, (LANES, LANES), 0)
@@ -266,11 +266,18 @@
             jnp.where(eye, line, 0.0), square, (((1,), (0,)), ((), ())),
             precision=lax.Precision.HIGHEST, preferred_element_type=jnp.float32)
 
+    span = ND // 2 if packed else ND
+    low_lanes = lax.broadcasted_iota(jnp.int32, (span, LANES), 1) < LANES // 2
+
     def prepare(freq, carry):
         at = PAD + freq * ND
         coef[0, freq, 0:ND, :] = 1.0 - jnp.abs(rates[pl.ds(at, ND), :])
         coef[1, freq, 0:ND, :] = jnp.maximum(rates[pl.ds(at - ND, ND), :], 0.0)
         coef[2, freq, 0:ND, :] = jnp.maximum(-rates[pl.ds(at + ND, ND), :], 0.0)
+        if packed:
+            for i in range(3):
+                coef[3 + i, freq, 0:span, :] = jnp.where(
+                    low_lanes, coef[i, freq, 0:span, :], coef[i, freq, span:ND, :])
         plus, minus = partners[0, freq * ND], partners[1, freq * ND]
         route[0, freq] = plus // ND
         route[1, freq] = plus - (plus // ND) * ND
@@ -283,27 +290,38 @@
     flat[0:PAD, :] = jnp.zeros((PAD, LANES), jnp.float32)
     flat[PAD + total :, :] = jnp.zeros((PAD, LANES), jnp.float32)
 
-    def spread(place, freq, values):
-        place[freq, EDGE : EDGE + ND, :] = values
-        place[freq, EDGE - WRAP : EDGE, :] = values[ND - WRAP :]
-        place[freq, EDGE + ND : EDGE + ND + WRAP, :] = values[:WRAP]
-
-    here = pl.ds(EDGE, ND)
-
     def settle(half):
+        width = span if half else ND
+        paired = packed and half == 1
+        here = pl.ds(EDGE, width)
+
+        def around(values):
+            return pltpu.roll(values, LANES // 2, 1) if paired else values
+
+        def spread(field, freq, values):
+            field[freq, EDGE : EDGE + width, :] = values
+            field[freq, EDGE - WRAP : EDGE, :] = around(values)[width - WRAP :]
+            field[freq, EDGE + width : EDGE + width + WRAP, :] = around(values)[:WRAP]
+
         def shift(freq, carry):
-            at = PAD + freq * ND
-            spread(wide, freq, coef[0, freq, 0:ND, :] * flat[pl.ds(at, ND), :]
-                   + coef[1, freq, 0:ND, :] * flat[pl.ds(at - ND, ND), :]
-                   + coef[2, freq, 0:ND, :] * flat[pl.ds(at + ND, ND), :])
+            at = PAD + freq * width
+            base = 3 if paired else 0
+            spread(wide, freq, coef[base, freq, 0:width, :] * flat[pl.ds(at, width), :]
+                   + coef[base + 1, freq, 0:width, :] * flat[pl.ds(at - width, width), :]
+                   + coef[base + 2, freq, 0:width, :] * flat[pl.ds(at + width, width), :])
             return carry
 
         def interact(freq, carry):
             value = wide[freq, here, :]
-            p = wide[route[0, freq], pl.ds(EDGE + route[1, freq], ND), :]
-            m = wide[route[2, freq], pl.ds(EDGE - route[3, freq], ND), :]
+            p = wide[route[0, freq], pl.ds(EDGE + route[1, freq], width), :]
+            m = wide[route[2, freq], pl.ds(EDGE - route[3, freq], width), :]
             spread(quartets, freq, value * (value * (p + m) - 2.0 * (p * m)))
             return carry
+
+        def settled(freq, values):
+            fresh[half, pl.ds(freq * ND, width), :] = values
+            if paired:
+                fresh[half, pl.ds(freq * ND + width, width), :] = around(values)
 
         def gather(freq, carry):
             source = -2.0 * quartets[freq, here, :]
@@ -311,78 +329,85 @@
                 f = jnp.maximum(freq - off, 0)
                 found = (route[0, f] == freq) & (freq >= off)
                 block = jnp.where(found, f, NF)
-                source = source + quartets[block, pl.ds(EDGE - route[1, f], ND), :]
+                source = source + quartets[block, pl.ds(EDGE - route[1, f], width), :]
                 f = jnp.minimum(freq + off, NF - 1)
                 found = (route[2, f] == freq) & (freq + off < NF)
                 block = jnp.where(found, f, NF)
-                source = source + quartets[block, pl.ds(EDGE + route[3, f], ND), :]
-            fresh[half, pl.ds(freq * ND, ND), :] = wide[freq, here, :] + dia_coeff * source
+                source = source + quartets[block, pl.ds(EDGE + route[3, f], width), :]
+            settled(freq, wide[freq, here, :] + dia_coeff * source)
             return carry
 
         lax.fori_loop(0, NF, shift, 0)
         lax.fori_loop(0, NF, interact, 0)
         lax.fori_loop(0, NF, gather, 0)
-        last = pl.ds((NF - 1) * ND, ND)
-        fresh[half, last, :] = fresh[half, last, :] + dia_coeff * (
-            quartets[NF - 1, pl.ds(EDGE - route[1, NF - 1], ND), :])
-        fresh[half, 0:ND, :] = fresh[half, 0:ND, :] + dia_coeff * (
-            quartets[0, pl.ds(EDGE + route[3, 0], ND), :])
-        save = pltpu.make_async_copy(fresh.at[half], fresh_out.at[half], out_sem.at[half])
-        save.start()
-        saves.append(save)
+        end = NF - 1
+        for freq, at in ((end, EDGE - route[1, end]), (0, EDGE + route[3, 0])):
+            extra = dia_coeff * quartets[freq, pl.ds(at, width), :]
+            settled(freq, fresh[half, freq * ND : freq * ND + width, :] + extra)
 
     def unpack_first(source, cells):
-        flat[pl.ds(PAD + source * n_chan, n_chan), :] = cells
+        at = PAD + source * n_chan
+        if not packed:
+            flat[pl.ds(at, n_chan), :] = cells[source]
+            return
+        wing = ND // 2
+        for freq in range(n_freq):
+            for w in range(2):
+                low = (freq // 2) * 2 * ND + w * ND + (freq % 2) * wing
+                flat[pl.ds(at + freq * ND + w * wing, wing), :] = cells[source, low : low + wing, :]
 
     def unpack_second(source, cells):
-        at = PAD + source * n_chan
-        if packed:
-            flat[pl.ds(at, part), :] = cells
-            flat[pl.ds(at + part, part), :] = pltpu.roll(cells, LANES // 2, 1)
-        else:
-            flat[pl.ds(at, n_chan), :] = cells
+        count = part if packed else n_chan
+        flat[pl.ds(PAD + source * count, count), :] = cells[source]
 
     def take_first(step, carry):
         source = lax.rem(me + n_spec - step, n_spec)
         for kind in kinds:
             sending(kind, step).wait_recv()
-        unpack_first(source, first_in[source])
+        unpack_first(source, first_in)
         return carry
 
     def take_second(step, carry):
         source = lax.rem(me + n_spec - step, n_spec)
-        sending(2, step).wait_recv()
-        unpack_second(source, second_in[source])
-        return carry
-
-    unpack_first(me, first[me])
+        sending(last_kind, step).wait_recv()
+        unpack_second(source, second_in)
+        return carry
+
+    unpack_first(me, first)
     lax.fori_loop(1, n_spec, take_first, 0)
     settle(0)
-    unpack_second(me, second[me])
+    if packed:
+        flat[PAD + total // 2 : 2 * PAD + total // 2, :] = jnp.zeros((PAD, LANES), jnp.float32)
+    unpack_second(me, second)
     lax.fori_loop(1, n_spec, take_second, 0)
     settle(1)
 
     def finish(step, carry):
-        for kind in kinds + (2,):
+        for kind in kinds + (last_kind,):
             sending(kind, step).wait_send()
         return carry
 
-    lax.fori_loop(1, n_spec, finish, 0)
-    for save in saves:
-        save.wait()
-
-
-def expand_kernel(fresh, spots, out):
+    def saving(chunk):
+        rows = pl.ds(pl.multiple_of(chunk * 2 * LANES, 2 * LANES), 2 * LANES)
+        return pltpu.make_async_copy(whole_out.at[rows], out.at[rows], out_sem.at[chunk])
+
     def expand(chunk, carry):
         rows = pl.ds(pl.multiple_of(chunk * LANES, LANES), LANES)
         values = jnp.concatenate([fresh[0, rows, :], fresh[1, rows, :]], axis=1)
-        cells = picked(values, spots[...], ((1,), (1,)))
+        cells = picked(values, spots[...], ((1,), (0,)))
         for r in range(2):
-            out[pl.ds(chunk * 2 * LANES + r, LANES, stride=2), :] = (
+            whole_out[pl.ds(chunk * 2 * LANES + r, LANES, stride=2), :] = (
                 cells[:, r * LANES : (r + 1) * LANES])
-        return carry
-
-    lax.fori_loop(0, fresh.shape[1] // LANES, expand, 0)
+        saving(chunk).start()
+        return carry
+
+    def saved(chunk, carry):
+        saving(chunk).wait()
+        return carry
+
+    lax.fori_loop(0, total // LANES, expand, 0)
+    lax.fori_loop(1, n_spec, finish, 0)
+    lax.fori_loop(0, total // LANES, saved, 0)
 
 
 def shards(spectrum, depth_speed, turning, drift, partners, sea_slots, sea_counts):
@@ -392,15 +417,15 @@
     packed = n_chan % 16 == 0 and n_chan // ND % 2 == 0 and cap <= 3 * LANES // 2
     n_freq = n_chan // ND
     rest = n_chan // 2 if packed else n_chan
+    kinds = n_chan // (2 * ND) + 1 if packed else 2
     total = ND * NF
     f32 = jnp.float32
     hbm = pl.BlockSpec(memory_space=pltpu.HBM)
-    fresh, spots = pl.pallas_call(
+    settled = pl.pallas_call(
         functools.partial(step_kernel, packed, n_spec, n_tile, grid_rows, n_chan),
-        out_shape=(jax.ShapeDtypeStruct((2, total, LANES), f32),
-                   jax.ShapeDtypeStruct((2 * LANES, 2 * LANES), jnp.bfloat16)),
+        out_shape=jax.ShapeDtypeStruct((2 * total, LANES), f32),
         in_specs=[hbm] * 7,
-        out_specs=(hbm, hbm),
+        out_specs=hbm,
         scratch_shapes=[
             pltpu.VMEM((n_chan * grid_rows, LANES), f32),
             pltpu.VMEM((grid_rows, LANES), f32),
@@ -411,7 +436,7 @@
             pltpu.SMEM((1, n_spec), jnp.int32),
             pltpu.SemaphoreType.DMA((7,)),
             pltpu.VMEM((n_spec, 1, 2 * LANES), jnp.int32),
-            pltpu.VMEM((n_spec, 2 * LANES, (3 if packed else 2) * LANES), jnp.bfloat16),
+            pltpu.VMEM((n_spec, 2 * LANES, 2 * LANES), jnp.bfloat16),
             pltpu.VMEM((grid_rows, LANES), f32),
             pltpu.VMEM((n_freq, grid_rows, LANES), f32),
             pltpu.VMEM((2, n_freq, grid_rows, LANES), f32),
@@ -422,33 +447,25 @@
             pltpu.VMEM((n_spec, n_chan, LANES), f32),
             pltpu.VMEM((n_spec, rest, LANES), f32),
             pltpu.VMEM((total + 2 * PAD, LANES), f32),
-            pltpu.VMEM((3, NF, PAD, LANES), f32),
+            pltpu.VMEM((6, NF, PAD, LANES), f32),
             pltpu.VMEM((total + 2 * PAD, LANES), f32),
             pltpu.VMEM((NF, ROWS, LANES), f32),
             pltpu.VMEM((NF + 1, ROWS, LANES), f32),
             pltpu.SMEM((4, NF), jnp.int32),
             pltpu.VMEM((2, total, LANES), f32),
-            pltpu.SemaphoreType.DMA((3,)),
+            pltpu.VMEM((2 * total, LANES), f32),
+            pltpu.VMEM((2 * LANES, 2 * LANES), jnp.bfloat16),
+            pltpu.VMEM((LANES, 2 * LANES), f32),
+            pltpu.SemaphoreType.DMA((total // LANES,)),
             pltpu.SemaphoreType.DMA((2,)),
             pltpu.SemaphoreType.DMA((2,)),
-            pltpu.SemaphoreType.DMA((3, n_spec)),
-            pltpu.SemaphoreType.DMA((3, n_spec)),
+            pltpu.SemaphoreType.DMA((kinds, n_spec)),
+            pltpu.SemaphoreType.DMA((kinds, n_spec)),
         ],
         compiler_params=pltpu.CompilerParams(
             collective_id=0, has_side_effects=True, vmem_limit_bytes=VMEM_ALL),
     )(spectrum.reshape(n_chan * grid_rows, grid_cols), depth_speed, turning, drift,
       partners, sea_slots, sea_counts.T)
-    settled = pl.pallas_call(
-        expand_kernel,
-        out_shape=jax.ShapeDtypeStruct((total * 2, LANES), f32),
-        grid=(PARTS,),
-        in_specs=[
-            pl.BlockSpec((2, total // PARTS, LANES), lambda i: (0, i, 0)),
-            pl.BlockSpec((2 * LANES, 2 * LANES), lambda i: (0, 0)),
-        ],
-        out_specs=pl.BlockSpec((2 * total // PARTS, LANES), lambda i: (i, 0)),
-        compiler_params=pltpu.CompilerParams(vmem_limit_bytes=VMEM_ALL),
-    )(fresh, spots)
     return settled.reshape(total, 2, LANES)
 
 

time: 30.4 us -> 33.8 us (1.11)
  local copies, waits for them, and re-layouts: 0 us -> 2.12 us
  Pallas kernels: 30.2 us -> 31.5 us
    pallas_call x1, Pallas kernels: 25.9 us -> 31.5 us  [shards(): pl.pallas_call(functools.partial(step_kernel, packed, n_spec, n_tile, gri...]
    pallas_call x1 -> x0, Pallas kernels: 4.29 us -> none  [shards(): pl.pallas_call(expand_kernel, out_shape=jax.ShapeDtypeStruct((total * 2,...]
    unnamed x0 -> x1, local copies, waits for them, and re-layouts: none -> 2.12 us
where the time goes in v3:
time: 33.8 us; the launch traced here: 33.6 us
  Pallas kernels  31.5 us (93%)
  local copies, waits for them, and re-layouts  2.12 us (6%)
    pallas_call x1, Pallas kernels, shards(): pl.pallas_call(functools.partial(step_kernel, packed, n_spec, n_tile, gri...  31.5 us
    unnamed x1, local copies, waits for them, and re-layouts  2.12 us

profile of v3, /device:TPU:1, one launch (start us, length us, event | category | flops | bytes accessed | tf_op | source)
XLA Modules:
  0.0 33.6 jit_solution(5867529653439646845)
XLA Ops:
  0.0 31.5 %shard_map.73 = f32[2304,128]{1,0:T(8,128)} custom-call(f32[2304,128]{1,0:T(8,128)} %bitcast.4, f32[16,128]{1,0:T(8,128)} %depth_in.1, f32[16,128]{1,0:T(8,128)} %turning_in.1, f32[1152]{0:T(1024)} %drift_in.1, s32[2,1152]{1,0:T(2,128)} %partners_in.1, s32[8,1,192]{2,1,0:T(1,128)} %slots_in.1, s32[1,8]{1,0:T(1,128)} %bitcast.5), custom_call_target="tpu_custom_call" | custom-call | tf_op jit(solution)/shard_map/pallas_call | solution.py:424
  31.5 2.1 %copy.9 = f32[1152,2,128]{2,1,0:T(2,128)} copy(f32[1152,2,128]{2,1,0:T(2,128)} %bitcast.3) | data formatting | bytes 2359296

commit v4 on v3

--- a/solution.py
+++ b/solution.py
@@ -15,6 +15,8 @@
 EDGE = 8
 ROWS = 48
 PAD = 40
+PARTS = 3
+GROUP = 4
 VMEM_ALL = 64 * 2**20
 
 speed_top = 0.6
@@ -47,11 +49,11 @@
 
 def step_kernel(packed, n_spec, n_tile, grid_rows, n_chan,
                 spectrum_in, depth_in, turning_in, drift_in, partners_in, slots_in, counts_in,
-                out,
+                fresh_out, spots_out,
                 energy, depth, turning, drift, partners, slots, counts, in_sem,
                 slot_rows, table, mask, edge, halo, spaced, turned,
                 first, second, first_in, second_in,
-                rates, coef, flat, wide, quartets, route, fresh, whole_out, spots, lists, out_sem,
+                rates, coef, flat, wide, quartets, route, fresh, spots, lists, out_sem,
                 halo_send, halo_recv, send_sem, recv_sem):
     me = lax.axis_index("spec")
     tile = lax.axis_index("tile")
@@ -204,25 +206,32 @@
             src_ref=src, dst_ref=dst, send_sem=send_sem.at[kind, step],
             recv_sem=recv_sem.at[kind, step], device_id=(peer, tile), device_id_type=MESH)
 
-    def fill_pair(pair, block):
-        both = picked(cells_of(block, pair * 2 * ND, 2 * ND), table[block], ((1,), (0,)))
-        first[block, pair * 2 * ND : (pair + 1) * 2 * ND, :] = both[:, :LANES]
-        rest = both[:, LANES:]
-        second[block, pair * ND : (pair + 1) * ND, :] = (
-            rest[:ND] + pltpu.roll(rest, LANES // 2, 1)[ND:])
-
-    def fill_whole(block):
-        both = picked(cells_of(block, 0, n_chan), table[block], ((1,), (0,)))
-        first[block] = both[:, :LANES]
-        second[block] = both[:, LANES:]
+    def fill_pair(pair, blocks):
+        both = [picked(cells_of(block, pair * 2 * ND, 2 * ND), table[block], ((1,), (0,)))
+                for block in blocks]
+        for block, found in zip(blocks, both):
+            first[block, pair * 2 * ND : (pair + 1) * 2 * ND, :] = found[:, :LANES]
+            rest = found[:, LANES:]
+            second[block, pair * ND : (pair + 1) * ND, :] = (
+                rest[:ND] + pltpu.roll(rest, LANES // 2, 1)[ND:])
+
+    def fill_whole(blocks):
+        for block in blocks:
+            both = picked(cells_of(block, 0, n_chan), table[block], ((1,), (0,)))
+            first[block] = both[:, :LANES]
+            second[block] = both[:, LANES:]
 
     def stage(fill, kind):
-        def body(step, carry):
-            fill(lax.rem(me + step, n_spec))
-            sending(kind, step).start()
+        def body(group, carry):
+            steps = (2 * group + 1, 2 * group + 2)
+            fill([lax.rem(me + step, n_spec) for step in steps])
+            for step in steps:
+                sending(kind, step).start()
             return carry
 
-        lax.fori_loop(1, n_spec, body, 0)
+        lax.fori_loop(0, n_spec // 2 - 1, body, 0)
+        fill([lax.rem(me + n_spec - 1, n_spec), me])
+        sending(kind, n_spec - 1).start()
 
     def start_second(step, carry):
         sending(last_kind, step).start()
@@ -241,30 +250,29 @@
             lax.fori_loop(2 * pair, 2 * pair + 2, turn_all, 0)
             stage(functools.partial(fill_pair, pair), pair)
         lax.fori_loop(1, n_spec, start_second, 0)
-        for pair in range(last_kind):
-            fill_pair(pair, me)
     else:
         lax.fori_loop(0, n_freq, advect, 0)
         arrive()
         lax.fori_loop(0, n_freq, turn_all, 0)
         stage(fill_whole, 0)
         lax.fori_loop(1, n_spec, start_second, 0)
-        fill_whole(me)
     kinds = tuple(range(last_kind))
 
     spots[...] = jnp.transpose(table[me].astype(jnp.float32)).astype(jnp.bfloat16)
+    saves = [pltpu.make_async_copy(spots, spots_out, out_sem.at[2])]
+    saves[0].start()
     loads[5].wait()
     loads[6].wait()
-    eye = (lax.broadcasted_iota(jnp.int32, (LANES, LANES), 0)
-           == lax.broadcasted_iota(jnp.int32, (LANES, LANES), 1))
-    square = jnp.ones((LANES, LANES), jnp.float32)
     rates[0:PAD, :] = jnp.zeros((PAD, LANES), jnp.float32)
     rates[PAD + total :, :] = jnp.zeros((PAD, LANES), jnp.float32)
+    lists[0:LANES, 0:LANES] = jnp.zeros((LANES, LANES), jnp.float32)
     for chunk in range(total // LANES):
         line = drift[pl.ds(chunk * LANES, LANES)].reshape(1, LANES)
-        rates[PAD + chunk * LANES : PAD + (chunk + 1) * LANES, :] = lax.dot_general(
-            jnp.where(eye, line, 0.0), square, (((1,), (0,)), ((), ())),
-            precision=lax.Precision.HIGHEST, preferred_element_type=jnp.float32)
+        lists[chunk : chunk + 1, 0:LANES] = line
+    lines = jnp.transpose(lists[:, 0:LANES])
+    for chunk in range(total // LANES):
+        rates[PAD + chunk * LANES : PAD + (chunk + 1) * LANES, :] = jnp.broadcast_to(
+            lines[:, chunk : chunk + 1], (LANES, LANES))
 
     span = ND // 2 if packed else ND
     low_lanes = lax.broadcasted_iota(jnp.int32, (span, LANES), 1) < LANES // 2
@@ -303,27 +311,20 @@
             field[freq, EDGE - WRAP : EDGE, :] = around(values)[width - WRAP :]
             field[freq, EDGE + width : EDGE + width + WRAP, :] = around(values)[:WRAP]
 
-        def shift(freq, carry):
+        def shifted(freq):
             at = PAD + freq * width
             base = 3 if paired else 0
-            spread(wide, freq, coef[base, freq, 0:width, :] * flat[pl.ds(at, width), :]
-                   + coef[base + 1, freq, 0:width, :] * flat[pl.ds(at - width, width), :]
-                   + coef[base + 2, freq, 0:width, :] * flat[pl.ds(at + width, width), :])
-            return carry
-
-        def interact(freq, carry):
+            return (coef[base, freq, 0:width, :] * flat[pl.ds(at, width), :]
+                    + coef[base + 1, freq, 0:width, :] * flat[pl.ds(at - width, width), :]
+                    + coef[base + 2, freq, 0:width, :] * flat[pl.ds(at + width, width), :])
+
+        def interacted(freq):
             value = wide[freq, here, :]
             p = wide[route[0, freq], pl.ds(EDGE + route[1, freq], width), :]
             m = wide[route[2, freq], pl.ds(EDGE - route[3, freq], width), :]
-            spread(quartets, freq, value * (value * (p + m) - 2.0 * (p * m)))
-            return carry
-
-        def settled(freq, values):
-            fresh[half, pl.ds(freq * ND, width), :] = values
-            if paired:
-                fresh[half, pl.ds(freq * ND + width, width), :] = around(values)
-
-        def gather(freq, carry):
+            return value * (value * (p + m) - 2.0 * (p * m))
+
+        def gathered(freq):
             source = -2.0 * quartets[freq, here, :]
             for off in (1, 2, 3):
                 f = jnp.maximum(freq - off, 0)
@@ -334,16 +335,32 @@
                 found = (route[2, f] == freq) & (freq + off < NF)
                 block = jnp.where(found, f, NF)
                 source = source + quartets[block, pl.ds(EDGE + route[3, f], width), :]
-            settled(freq, wide[freq, here, :] + dia_coeff * source)
-            return carry
-
-        lax.fori_loop(0, NF, shift, 0)
-        lax.fori_loop(0, NF, interact, 0)
-        lax.fori_loop(0, NF, gather, 0)
+            return wide[freq, here, :] + dia_coeff * source
+
+        def settled(freq, values):
+            fresh[half, pl.ds(freq * ND, width), :] = values
+            if paired:
+                fresh[half, pl.ds(freq * ND + width, width), :] = around(values)
+
+        def every(get, put):
+            def body(step, carry):
+                freqs = [step * GROUP + i for i in range(GROUP)]
+                for freq, values in [(freq, get(freq)) for freq in freqs]:
+                    put(freq, values)
+                return carry
+
+            lax.fori_loop(0, NF // GROUP, body, 0)
+
+        every(shifted, functools.partial(spread, wide))
+        every(interacted, functools.partial(spread, quartets))
+        every(gathered, settled)
         end = NF - 1
         for freq, at in ((end, EDGE - route[1, end]), (0, EDGE + route[3, 0])):
             extra = dia_coeff * quartets[freq, pl.ds(at, width), :]
             settled(freq, fresh[half, freq * ND : freq * ND + width, :] + extra)
+        save = pltpu.make_async_copy(fresh.at[half], fresh_out.at[half], out_sem.at[half])
+        save.start()
+        saves.append(save)
 
     def unpack_first(source, cells):
         at = PAD + source * n_chan
@@ -387,27 +404,35 @@
             sending(kind, step).wait_send()
         return carry
 
-    def saving(chunk):
-        rows = pl.ds(pl.multiple_of(chunk * 2 * LANES, 2 * LANES), 2 * LANES)
-        return pltpu.make_async_copy(whole_out.at[rows], out.at[rows], out_sem.at[chunk])
-
-    def expand(chunk, carry):
-        rows = pl.ds(pl.multiple_of(chunk * LANES, LANES), LANES)
+    lax.fori_loop(1, n_spec, finish, 0)
+    for save in saves:
+        save.wait()
+
+
+def expand_kernel(fresh_in, spots_in, out, fresh, spots, cells, in_sem, out_sem):
+    total = fresh_in.shape[1]
+    size = total // PARTS
+    loads = [pltpu.make_async_copy(spots_in, spots, in_sem.at[PARTS])]
+    for i in range(PARTS):
+        rows = pl.ds(i * size, size)
+        loads.append(pltpu.make_async_copy(fresh_in.at[:, rows], fresh.at[:, rows], in_sem.at[i]))
+    for load in loads:
+        load.start()
+    loads[0].wait()
+    saves = []
+    for i in range(PARTS):
+        rows = pl.ds(i * size, size)
+        loads[i + 1].wait()
         values = jnp.concatenate([fresh[0, rows, :], fresh[1, rows, :]], axis=1)
-        cells = picked(values, spots[...], ((1,), (0,)))
+        found = picked(values, spots[...], ((1,), (0,)))
         for r in range(2):
-            whole_out[pl.ds(chunk * 2 * LANES + r, LANES, stride=2), :] = (
-                cells[:, r * LANES : (r + 1) * LANES])
-        saving(chunk).start()
-        return carry
-
-    def saved(chunk, carry):
-        saving(chunk).wait()
-        return carry
-
-    lax.fori_loop(0, total // LANES, expand, 0)
-    lax.fori_loop(1, n_spec, finish, 0)
-    lax.fori_loop(0, total // LANES, saved, 0)
+            cells[pl.ds(2 * i * size + r, size, stride=2), :] = found[:, r * LANES : (r + 1) * LANES]
+        rows = pl.ds(2 * i * size, 2 * size)
+        save = pltpu.make_async_copy(cells.at[rows], out.at[rows], out_sem.at[i])
+        save.start()
+        saves.append(save)
+    for save in saves:
+        save.wait()
 
 
 def shards(spectrum, depth_speed, turning, drift, partners, sea_slots, sea_counts):
@@ -421,11 +446,12 @@
     total = ND * NF
     f32 = jnp.float32
     hbm = pl.BlockSpec(memory_space=pltpu.HBM)
-    settled = pl.pallas_call(
+    fresh, spots = pl.pallas_call(
         functools.partial(step_kernel, packed, n_spec, n_tile, grid_rows, n_chan),
-        out_shape=jax.ShapeDtypeStruct((2 * total, LANES), f32),
+        out_shape=(jax.ShapeDtypeStruct((2, total, LANES), f32),
+                   jax.ShapeDtypeStruct((2 * LANES, 2 * LANES), jnp.bfloat16)),
         in_specs=[hbm] * 7,
-        out_specs=hbm,
+        out_specs=(hbm, hbm),
         scratch_shapes=[
             pltpu.VMEM((n_chan * grid_rows, LANES), f32),
             pltpu.VMEM((grid_rows, LANES), f32),
@@ -453,10 +479,9 @@
             pltpu.VMEM((NF + 1, ROWS, LANES), f32),
             pltpu.SMEM((4, NF), jnp.int32),
             pltpu.VMEM((2, total, LANES), f32),
-            pltpu.VMEM((2 * total, LANES), f32),
             pltpu.VMEM((2 * LANES, 2 * LANES), jnp.bfloat16),
             pltpu.VMEM((LANES, 2 * LANES), f32),
-            pltpu.SemaphoreType.DMA((total // LANES,)),
+            pltpu.SemaphoreType.DMA((3,)),
             pltpu.SemaphoreType.DMA((2,)),
             pltpu.SemaphoreType.DMA((2,)),
             pltpu.SemaphoreType.DMA((kinds, n_spec)),
@@ -466,6 +491,20 @@
             collective_id=0, has_side_effects=True, vmem_limit_bytes=VMEM_ALL),
     )(spectrum.reshape(n_chan * grid_rows, grid_cols), depth_speed, turning, drift,
       partners, sea_slots, sea_counts.T)
+    settled = pl.pallas_call(
+        expand_kernel,
+        out_shape=jax.ShapeDtypeStruct((total * 2, LANES), f32),
+        in_specs=[hbm, hbm],
+        out_specs=hbm,
+        scratch_shapes=[
+            pltpu.VMEM((2, total, LANES), f32),
+            pltpu.VMEM((2 * LANES, 2 * LANES), jnp.bfloat16),
+            pltpu.VMEM((total * 2, LANES), f32),
+            pltpu.SemaphoreType.DMA((PARTS + 1,)),
+            pltpu.SemaphoreType.DMA((PARTS,)),
+        ],
+        compiler_params=pltpu.CompilerParams(vmem_limit_bytes=VMEM_ALL),
+    )(fresh, spots)
     return settled.reshape(total, 2, LANES)
 
 

time: 33.8 us -> 27.4 us (0.81)
  Pallas kernels: 31.5 us -> 26.9 us
  local copies, waits for them, and re-layouts: 2.12 us -> 0 us
    pallas_call x1, Pallas kernels: 31.5 us -> 24.1 us  [shards(): pl.pallas_call(functools.partial(step_kernel, packed, n_spec, n_tile, gri...]
    pallas_call x0 -> x1, Pallas kernels: none -> 2.86 us  [shards(): pl.pallas_call(expand_kernel, out_shape=jax.ShapeDtypeStruct((total * 2,...]
    unnamed x1 -> x0, local copies, waits for them, and re-layouts: 2.12 us -> none
where the time goes in v4:
time: 27.4 us; the launch traced here: 26.9 us
  Pallas kernels  26.9 us (98%)
    pallas_call x1, Pallas kernels, shards(): pl.pallas_call(functools.partial(step_kernel, packed, n_spec, n_tile, gri...  24.1 us
    pallas_call x1, Pallas kernels, shards(): pl.pallas_call(expand_kernel, out_shape=jax.ShapeDtypeStruct((total * 2,...  2.86 us

profile of v4, /device:TPU:1, one launch (start us, length us, event | category | flops | bytes accessed | tf_op | source)
XLA Modules:
  0.0 26.9 jit_solution(9277884559144353174)
XLA Ops:
  0.0 24.1 %shard_map.73 = (f32[2,1152,128]{2,1,0:T(8,128)}, bf16[256,256]{1,0:T(8,128)(2,1)}) custom-call(f32[2304,128]{1,0:T(8,128)} %bitcast.3, f32[16,128]{1,0:T(8,128)} %depth_in.1, f32[16,128]{1,0:T(8,128)} %turning_in.1, f32[1152]{0:T(1024)} %drift_in.1, s32[2,1152]{1,0:T(2,128)} %partners_in.1, s32[8,1,192]{2,1,0:T(1,128)} %slots_in.1, s32[1,8]{1,0:T(1,128)} %bitcast.4), custom_call_target="tpu_custom_call" | custom-call | tf_op jit(solution)/shard_map/pallas_call | solution.py:449
  24.1 2.9 %shard_map.74 = f32[2304,128]{1,0:T(8,128)} custom-call(f32[2,1152,128]{2,1,0:T(8,128)} %get-tuple-element.7.fresh_in, bf16[256,256]{1,0:T(8,128)(2,1)} %get-tuple-element.8.spots_in), custom_call_target="tpu_custom_call" | custom-call | tf_op jit(solution)/shard_map/pallas_call | solution.py:494

commit v5 on v4

--- a/solution.py
+++ b/solution.py
@@ -15,7 +15,7 @@
 EDGE = 8
 ROWS = 48
 PAD = 40
-PARTS = 3
+PARTS = 6
 GROUP = 4
 VMEM_ALL = 64 * 2**20
 
@@ -25,6 +25,7 @@
 
 MESH = pl.DeviceIdType.MESH
 COS = [math.cos(2.0 * math.pi * d / ND) for d in range(ND)]
+FLOWS = ([d for d in range(ND) if COS[d] > 0], [d for d in range(ND) if COS[d] <= 0])
 SIN = [math.sin(2.0 * math.pi * d / ND) for d in range(ND)]
 
 
@@ -113,32 +114,36 @@
         return weight * (speed_top * jnp.exp(jnp.full((grid_rows, LANES), -decline * number)))
 
     def cell_rows(freq, direction):
-        start = pl.multiple_of((freq * ND + direction) * grid_rows, 8)
-        return pl.ds(start, grid_rows)
+        start = (freq * ND + direction) * grid_rows
+        return pl.ds(start if isinstance(start, int) else pl.multiple_of(start, 8), grid_rows)
 
     def placed(freq, direction):
         if not packed:
             return cell_rows(freq, direction)
         wing = ND // 2
-        at = (freq // 2) * 2 * ND + (direction // wing) * ND + lax.rem(freq, 2) * wing
-        return pl.ds(pl.multiple_of((at + direction % wing) * grid_rows, 8), grid_rows)
-
-    def make_edge(freq, carry):
+        at = (freq // 2) * 2 * ND + (direction // wing) * ND + (freq % 2) * wing
+        return pl.ds((at + direction % wing) * grid_rows, grid_rows)
+
+    def edge_lane(freq, direction):
+        side = 0 if COS[direction] > 0 else 1
+        return freq * len(FLOWS[side]) + FLOWS[side].index(direction)
+
+    held = [jnp.zeros((grid_rows, LANES), jnp.float32) for _ in FLOWS]
+    for freq in range(n_freq):
         rate = scaled(freq)
-        held = jnp.zeros((grid_rows, LANES), jnp.float32)
-        for d in range(ND):
-            flow = energy[cell_rows(freq, d), :] * rate
-            moved = pltpu.roll(flow, d + 1 if COS[d] > 0 else d, 1)
-            held = jnp.where(lane == d, moved, held)
-        edge[freq] = held
-        return carry
-
-    lax.fori_loop(0, n_freq, make_edge, 0)
+        for side, flows in enumerate(FLOWS):
+            for d in flows:
+                at = edge_lane(freq, d)
+                flow = energy[cell_rows(freq, d), :] * rate
+                moved = pltpu.roll(flow, (at + 1 - side) % LANES, 1)
+                held[side] = jnp.where(lane == at, moved, held[side])
+    for side in range(2):
+        edge[side] = held[side]
     pl.semaphore_wait(barrier, n_spec + 1)
     copies = []
     for place, neighbour in enumerate((right, left)):
         copy = pltpu.make_async_remote_copy(
-            src_ref=edge, dst_ref=halo.at[place], send_sem=halo_send.at[place],
+            src_ref=edge.at[place], dst_ref=halo.at[place], send_sem=halo_send.at[place],
             recv_sem=halo_recv.at[place], device_id=(me, neighbour), device_id_type=MESH)
         copy.start()
         copies.append(copy)
@@ -163,19 +168,18 @@
             spaced[cell_rows(freq, d), :] = result
         return carry
 
-    def turn_all(freq, carry):
+    def turn_all(freq):
         turn = turning[...]
         stay, ahead = 1.0 - jnp.abs(turn), jnp.maximum(turn, 0.0)
         back = jnp.maximum(-turn, 0.0)
 
         def whole(d):
             value = spaced[cell_rows(freq, d), :]
+            at = edge_lane(freq, d)
             if COS[d] > 0:
-                held = halo[0, freq]
-                moved = pltpu.roll(held, (LANES - d) % LANES, 1) if d else held
+                moved = pltpu.roll(halo[0], (LANES - at) % LANES, 1)
                 return value + jnp.where(lane == 0, COS[d] * moved, 0.0)
-            held = halo[1, freq]
-            moved = pltpu.roll(held, LANES - 1 - d, 1)
+            moved = pltpu.roll(halo[1], LANES - 1 - at, 1)
             return value + jnp.where(lane == LANES - 1, -COS[d] * moved, 0.0)
 
         start = whole(0)
@@ -184,7 +188,6 @@
             after = whole(d + 1) if d + 1 < ND else start
             turned[placed(freq, d), :] = stay * here + ahead * before + back * after
             before, here = here, after
-        return carry
 
     def cells_of(block, low, count):
         return jnp.concatenate(
@@ -242,18 +245,17 @@
             copy.wait()
         loads[4].wait()
 
+    lax.fori_loop(0, n_freq, advect, 0)
+    arrive()
     if packed:
         for pair in range(last_kind):
-            lax.fori_loop(2 * pair, 2 * pair + 2, advect, 0)
-            if pair == 0:
-                arrive()
-            lax.fori_loop(2 * pair, 2 * pair + 2, turn_all, 0)
+            turn_all(2 * pair)
+            turn_all(2 * pair + 1)
             stage(functools.partial(fill_pair, pair), pair)
         lax.fori_loop(1, n_spec, start_second, 0)
     else:
-        lax.fori_loop(0, n_freq, advect, 0)
-        arrive()
-        lax.fori_loop(0, n_freq, turn_all, 0)
+        for freq in range(n_freq):
+            turn_all(freq)
         stage(fill_whole, 0)
         lax.fori_loop(1, n_spec, start_second, 0)
     kinds = tuple(range(last_kind))
@@ -464,8 +466,8 @@
             pltpu.VMEM((n_spec, 1, 2 * LANES), jnp.int32),
             pltpu.VMEM((n_spec, 2 * LANES, 2 * LANES), jnp.bfloat16),
             pltpu.VMEM((grid_rows, LANES), f32),
-            pltpu.VMEM((n_freq, grid_rows, LANES), f32),
-            pltpu.VMEM((2, n_freq, grid_rows, LANES), f32),
+            pltpu.VMEM((2, grid_rows, LANES), f32),
+            pltpu.VMEM((2, grid_rows, LANES), f32),
             pltpu.VMEM((n_chan * grid_rows, LANES), f32),
             pltpu.VMEM((n_chan * grid_rows, LANES), f32),
             pltpu.VMEM((n_spec, n_chan, LANES), f32),

time: 27.4 us -> 27.1 us (0.989)
    pallas_call x1, Pallas kernels: 24.1 us -> 23.5 us  [shards(): pl.pallas_call(functools.partial(step_kernel, packed, n_spec, n_tile, gri...]
    pallas_call x1, Pallas kernels: 2.86 us -> 3.29 us  [shards(): pl.pallas_call(expand_kernel, out_shape=jax.ShapeDtypeStruct((total * 2,...]
where the time goes in v5:
time: 27.1 us; the launch traced here: 26.8 us
  Pallas kernels  26.8 us (99%)
    pallas_call x1, Pallas kernels, shards(): pl.pallas_call(functools.partial(step_kernel, packed, n_spec, n_tile, gri...  23.5 us
    pallas_call x1, Pallas kernels, shards(): pl.pallas_call(expand_kernel, out_shape=jax.ShapeDtypeStruct((total * 2,...  3.29 us

profile of v5, /device:TPU:1, one launch (start us, length us, event | category | flops | bytes accessed | tf_op | source)
XLA Modules:
  0.0 26.8 jit_solution(8515627551111979279)
XLA Ops:
  0.0 23.5 %shard_map.73 = (f32[2,1152,128]{2,1,0:T(8,128)}, bf16[256,256]{1,0:T(8,128)(2,1)}) custom-call(f32[2304,128]{1,0:T(8,128)} %bitcast.3, f32[16,128]{1,0:T(8,128)} %depth_in.1, f32[16,128]{1,0:T(8,128)} %turning_in.1, f32[1152]{0:T(1024)} %drift_in.1, s32[2,1152]{1,0:T(2,128)} %partners_in.1, s32[8,1,192]{2,1,0:T(1,128)} %slots_in.1, s32[1,8]{1,0:T(1,128)} %bitcast.4), custom_call_target="tpu_custom_call" | custom-call | tf_op jit(solution)/shard_map/pallas_call | solution.py:451
  23.5 3.3 %shard_map.74 = f32[2304,128]{1,0:T(8,128)} custom-call(f32[2,1152,128]{2,1,0:T(8,128)} %get-tuple-element.7.fresh_in, bf16[256,256]{1,0:T(8,128)(2,1)} %get-tuple-element.8.spots_in), custom_call_target="tpu_custom_call" | custom-call | tf_op jit(solution)/shard_map/pallas_call | solution.py:496

commit v6 on v5

--- a/solution.py
+++ b/solution.py
@@ -15,8 +15,8 @@
 EDGE = 8
 ROWS = 48
 PAD = 40
-PARTS = 6
-GROUP = 4
+PARTS = 2
+GROUP = 8
 VMEM_ALL = 64 * 2**20
 
 speed_top = 0.6
@@ -54,7 +54,7 @@
                 energy, depth, turning, drift, partners, slots, counts, in_sem,
                 slot_rows, table, mask, edge, halo, spaced, turned,
                 first, second, first_in, second_in,
-                rates, coef, flat, wide, quartets, route, fresh, spots, lists, out_sem,
+                rates, coef, flat, wide, quartets, route, rows, fresh, spots, lists, out_sem,
                 halo_send, halo_recv, send_sem, recv_sem):
     me = lax.axis_index("spec")
     tile = lax.axis_index("tile")
@@ -201,8 +201,8 @@
         if kind == last_kind:
             src, dst = second.at[peer], second_in.at[me]
         elif packed:
-            rows = pl.ds(kind * 2 * ND, 2 * ND)
-            src, dst = first.at[peer, rows], first_in.at[me, rows]
+            part_rows = pl.ds(kind * 2 * ND, 2 * ND)
+            src, dst = first.at[peer, part_rows], first_in.at[me, part_rows]
         else:
             src, dst = first.at[peer], first_in.at[me]
         return pltpu.make_async_remote_copy(
@@ -295,23 +295,38 @@
         route[3, freq] = lax.rem(ND - (minus - (minus // ND) * ND), ND)
         return carry
 
+    def find_rows(freq, carry):
+        rows[0, freq] = route[0, freq] * ROWS + EDGE + route[1, freq]
+        rows[1, freq] = route[2, freq] * ROWS + EDGE - route[3, freq]
+        for off in (1, 2, 3):
+            f = jnp.maximum(freq - off, 0)
+            found = (route[0, f] == freq) & (freq >= off)
+            rows[2 * off, freq] = jnp.where(found, f, NF) * ROWS + EDGE - route[1, f]
+            f = jnp.minimum(freq + off, NF - 1)
+            found = (route[2, f] == freq) & (freq + off < NF)
+            rows[2 * off + 1, freq] = jnp.where(found, f, NF) * ROWS + EDGE + route[3, f]
+        return carry
+
     lax.fori_loop(0, NF, prepare, 0)
-    quartets[NF] = jnp.zeros((ROWS, LANES), jnp.float32)
+    lax.fori_loop(0, NF, find_rows, 0)
+    quartets[NF * ROWS :, :] = jnp.zeros((ROWS, LANES), jnp.float32)
     flat[0:PAD, :] = jnp.zeros((PAD, LANES), jnp.float32)
     flat[PAD + total :, :] = jnp.zeros((PAD, LANES), jnp.float32)
 
     def settle(half):
         width = span if half else ND
         paired = packed and half == 1
-        here = pl.ds(EDGE, width)
+
+        def home(freq, shift=0, count=width):
+            return pl.ds(freq * ROWS + EDGE + shift, count)
 
         def around(values):
             return pltpu.roll(values, LANES // 2, 1) if paired else values
 
         def spread(field, freq, values):
-            field[freq, EDGE : EDGE + width, :] = values
-            field[freq, EDGE - WRAP : EDGE, :] = around(values)[width - WRAP :]
-            field[freq, EDGE + width : EDGE + width + WRAP, :] = around(values)[:WRAP]
+            field[home(freq), :] = values
+            field[home(freq, -WRAP, WRAP), :] = around(values)[width - WRAP :]
+            field[home(freq, width, WRAP), :] = around(values)[:WRAP]
 
         def shifted(freq):
             at = PAD + freq * width
@@ -321,23 +336,15 @@
                     + coef[base + 2, freq, 0:width, :] * flat[pl.ds(at + width, width), :])
 
         def interacted(freq):
-            value = wide[freq, here, :]
-            p = wide[route[0, freq], pl.ds(EDGE + route[1, freq], width), :]
-            m = wide[route[2, freq], pl.ds(EDGE - route[3, freq], width), :]
+            value = wide[home(freq), :]
+            p, m = wide[pl.ds(rows[0, freq], width), :], wide[pl.ds(rows[1, freq], width), :]
             return value * (value * (p + m) - 2.0 * (p * m))
 
         def gathered(freq):
-            source = -2.0 * quartets[freq, here, :]
-            for off in (1, 2, 3):
-                f = jnp.maximum(freq - off, 0)
-                found = (route[0, f] == freq) & (freq >= off)
-                block = jnp.where(found, f, NF)
-                source = source + quartets[block, pl.ds(EDGE - route[1, f], width), :]
-                f = jnp.minimum(freq + off, NF - 1)
-                found = (route[2, f] == freq) & (freq + off < NF)
-                block = jnp.where(found, f, NF)
-                source = source + quartets[block, pl.ds(EDGE + route[3, f], width), :]
-            return wide[freq, here, :] + dia_coeff * source
+            source = -2.0 * quartets[home(freq), :]
+            for i in range(2, 8):
+                source = source + quartets[pl.ds(rows[i, freq], width), :]
+            return wide[home(freq), :] + dia_coeff * source
 
         def settled(freq, values):
             fresh[half, pl.ds(freq * ND, width), :] = values
@@ -357,8 +364,8 @@
         every(interacted, functools.partial(spread, quartets))
         every(gathered, settled)
         end = NF - 1
-        for freq, at in ((end, EDGE - route[1, end]), (0, EDGE + route[3, 0])):
-            extra = dia_coeff * quartets[freq, pl.ds(at, width), :]
+        for freq, shift in ((end, -route[1, end]), (0, route[3, 0])):
+            extra = dia_coeff * quartets[home(freq, shift), :]
             settled(freq, fresh[half, freq * ND : freq * ND + width, :] + extra)
         save = pltpu.make_async_copy(fresh.at[half], fresh_out.at[half], out_sem.at[half])
         save.start()
@@ -477,9 +484,10 @@
             pltpu.VMEM((total + 2 * PAD, LANES), f32),
             pltpu.VMEM((6, NF, PAD, LANES), f32),
             pltpu.VMEM((total + 2 * PAD, LANES), f32),
-            pltpu.VMEM((NF, ROWS, LANES), f32),
-            pltpu.VMEM((NF + 1, ROWS, LANES), f32),
+            pltpu.VMEM((NF * ROWS, LANES), f32),
+            pltpu.VMEM(((NF + 1) * ROWS, LANES), f32),
             pltpu.SMEM((4, NF), jnp.int32),
+            pltpu.SMEM((8, NF), jnp.int32),
             pltpu.VMEM((2, total, LANES), f32),
             pltpu.VMEM((2 * LANES, 2 * LANES), jnp.bfloat16),
             pltpu.VMEM((LANES, 2 * LANES), f32),

time: 27.1 us -> 25.5 us (0.941)
  Pallas kernels: 26.8 us -> 25.2 us
    pallas_call x1, Pallas kernels: 23.5 us -> 22.3 us  [shards(): pl.pallas_call(functools.partial(step_kernel, packed, n_spec, n_tile, gri...]
    pallas_call x1, Pallas kernels: 3.29 us -> 2.9 us  [shards(): pl.pallas_call(expand_kernel, out_shape=jax.ShapeDtypeStruct((total * 2,...]
where the time goes in v6:
time: 25.5 us; the launch traced here: 25.2 us
  Pallas kernels  25.2 us (99%)
    pallas_call x1, Pallas kernels, shards(): pl.pallas_call(functools.partial(step_kernel, packed, n_spec, n_tile, gri...  22.3 us
    pallas_call x1, Pallas kernels, shards(): pl.pallas_call(expand_kernel, out_shape=jax.ShapeDtypeStruct((total * 2,...  2.9 us

profile of v6, /device:TPU:1, one launch (start us, length us, event | category | flops | bytes accessed | tf_op | source)
XLA Modules:
  0.0 25.2 jit_solution(14030625441426642397)
XLA Ops:
  0.0 22.3 %shard_map.73 = (f32[2,1152,128]{2,1,0:T(8,128)}, bf16[256,256]{1,0:T(8,128)(2,1)}) custom-call(f32[2304,128]{1,0:T(8,128)} %bitcast.3, f32[16,128]{1,0:T(8,128)} %depth_in.1, f32[16,128]{1,0:T(8,128)} %turning_in.1, f32[1152]{0:T(1024)} %drift_in.1, s32[2,1152]{1,0:T(2,128)} %partners_in.1, s32[8,1,192]{2,1,0:T(1,128)} %slots_in.1, s32[1,8]{1,0:T(1,128)} %bitcast.4), custom_call_target="tpu_custom_call" | custom-call | tf_op jit(solution)/shard_map/pallas_call | solution.py:458
  22.3 2.9 %shard_map.74 = f32[2304,128]{1,0:T(8,128)} custom-call(f32[2,1152,128]{2,1,0:T(8,128)} %get-tuple-element.7.fresh_in, bf16[256,256]{1,0:T(8,128)(2,1)} %get-tuple-element.8.spots_in), custom_call_target="tpu_custom_call" | custom-call | tf_op jit(solution)/shard_map/pallas_call | solution.py:504

commit v7 on v6

--- a/solution.py
+++ b/solution.py
@@ -17,6 +17,7 @@
 PAD = 40
 PARTS = 2
 GROUP = 8
+BLOCKS = 4
 VMEM_ALL = 64 * 2**20
 
 speed_top = 0.6
@@ -226,15 +227,17 @@
 
     def stage(fill, kind):
         def body(group, carry):
-            steps = (2 * group + 1, 2 * group + 2)
+            steps = [BLOCKS * group + 1 + i for i in range(BLOCKS)]
             fill([lax.rem(me + step, n_spec) for step in steps])
             for step in steps:
                 sending(kind, step).start()
             return carry
 
-        lax.fori_loop(0, n_spec // 2 - 1, body, 0)
-        fill([lax.rem(me + n_spec - 1, n_spec), me])
-        sending(kind, n_spec - 1).start()
+        lax.fori_loop(0, n_spec // BLOCKS - 1, body, 0)
+        steps = range(n_spec - BLOCKS + 1, n_spec)
+        fill([lax.rem(me + step, n_spec) for step in steps] + [me])
+        for step in steps:
+            sending(kind, step).start()
 
     def start_second(step, carry):
         sending(last_kind, step).start()
@@ -261,8 +264,8 @@
     kinds = tuple(range(last_kind))
 
     spots[...] = jnp.transpose(table[me].astype(jnp.float32)).astype(jnp.bfloat16)
-    saves = [pltpu.make_async_copy(spots, spots_out, out_sem.at[2])]
-    saves[0].start()
+    spots_save = pltpu.make_async_copy(spots, spots_out, out_sem.at[2, 0])
+    spots_save.start()
     loads[5].wait()
     loads[6].wait()
     rates[0:PAD, :] = jnp.zeros((PAD, LANES), jnp.float32)
@@ -279,39 +282,68 @@
     span = ND // 2 if packed else ND
     low_lanes = lax.broadcasted_iota(jnp.int32, (span, LANES), 1) < LANES // 2
 
-    def prepare(freq, carry):
+    def every(get, put, after=None):
+        def body(step, carry):
+            freqs = [step * GROUP + i for i in range(GROUP)]
+            for freq, values in [(freq, get(freq)) for freq in freqs]:
+                put(freq, values)
+            if after is not None:
+                after(step)
+            return carry
+
+        lax.fori_loop(0, NF // GROUP, body, 0)
+
+    def get_coef(freq):
         at = PAD + freq * ND
-        coef[0, freq, 0:ND, :] = 1.0 - jnp.abs(rates[pl.ds(at, ND), :])
-        coef[1, freq, 0:ND, :] = jnp.maximum(rates[pl.ds(at - ND, ND), :], 0.0)
-        coef[2, freq, 0:ND, :] = jnp.maximum(-rates[pl.ds(at + ND, ND), :], 0.0)
-        if packed:
-            for i in range(3):
-                coef[3 + i, freq, 0:span, :] = jnp.where(
-                    low_lanes, coef[i, freq, 0:span, :], coef[i, freq, span:ND, :])
+        return (1.0 - jnp.abs(rates[pl.ds(at, ND), :]),
+                jnp.maximum(rates[pl.ds(at - ND, ND), :], 0.0),
+                jnp.maximum(-rates[pl.ds(at + ND, ND), :], 0.0))
+
+    def put_coef(freq, values):
+        for i, value in enumerate(values):
+            coef[i, freq, 0:ND, :] = value
+            if packed:
+                coef[3 + i, freq, 0:span, :] = jnp.where(low_lanes, value[:span], value[span:])
+
+    def get_route(freq):
         plus, minus = partners[0, freq * ND], partners[1, freq * ND]
-        route[0, freq] = plus // ND
-        route[1, freq] = plus - (plus // ND) * ND
-        route[2, freq] = minus // ND
-        route[3, freq] = lax.rem(ND - (minus - (minus // ND) * ND), ND)
-        return carry
-
-    def find_rows(freq, carry):
-        rows[0, freq] = route[0, freq] * ROWS + EDGE + route[1, freq]
-        rows[1, freq] = route[2, freq] * ROWS + EDGE - route[3, freq]
+        upper, lower = plus // ND, minus // ND
+        return (upper, plus - upper * ND, lower, lax.rem(ND - (minus - lower * ND), ND))
+
+    def put_route(freq, values):
+        for i, value in enumerate(values):
+            route[i, freq] = value
+
+    def get_rows(freq):
+        found_rows = [route[0, freq] * ROWS + EDGE + route[1, freq],
+                      route[2, freq] * ROWS + EDGE - route[3, freq]]
         for off in (1, 2, 3):
             f = jnp.maximum(freq - off, 0)
             found = (route[0, f] == freq) & (freq >= off)
-            rows[2 * off, freq] = jnp.where(found, f, NF) * ROWS + EDGE - route[1, f]
+            found_rows.append(jnp.where(found, f, NF) * ROWS + EDGE - route[1, f])
             f = jnp.minimum(freq + off, NF - 1)
             found = (route[2, f] == freq) & (freq + off < NF)
-            rows[2 * off + 1, freq] = jnp.where(found, f, NF) * ROWS + EDGE + route[3, f]
-        return carry
-
-    lax.fori_loop(0, NF, prepare, 0)
-    lax.fori_loop(0, NF, find_rows, 0)
+            found_rows.append(jnp.where(found, f, NF) * ROWS + EDGE + route[3, f])
+        end = NF - 1
+        own = jnp.where(freq == 0, EDGE + route[3, 0], NF * ROWS + EDGE)
+        found_rows.append(jnp.where(freq == end, end * ROWS + EDGE - route[1, end], own))
+        return found_rows
+
+    def put_rows(freq, values):
+        for i, value in enumerate(values):
+            rows[i, freq] = value
+
+    every(get_coef, put_coef)
+    every(get_route, put_route)
+    every(get_rows, put_rows)
     quartets[NF * ROWS :, :] = jnp.zeros((ROWS, LANES), jnp.float32)
     flat[0:PAD, :] = jnp.zeros((PAD, LANES), jnp.float32)
     flat[PAD + total :, :] = jnp.zeros((PAD, LANES), jnp.float32)
+
+    def saving(half, step):
+        at = pl.ds(pl.multiple_of(step * GROUP * ND, 8), GROUP * ND)
+        return pltpu.make_async_copy(
+            fresh.at[half, at], fresh_out.at[half, at], out_sem.at[half, step])
 
     def settle(half):
         width = span if half else ND
@@ -342,7 +374,7 @@
 
         def gathered(freq):
             source = -2.0 * quartets[home(freq), :]
-            for i in range(2, 8):
+            for i in range(2, 9):
                 source = source + quartets[pl.ds(rows[i, freq], width), :]
             return wide[home(freq), :] + dia_coeff * source
 
@@ -351,25 +383,9 @@
             if paired:
                 fresh[half, pl.ds(freq * ND + width, width), :] = around(values)
 
-        def every(get, put):
-            def body(step, carry):
-                freqs = [step * GROUP + i for i in range(GROUP)]
-                for freq, values in [(freq, get(freq)) for freq in freqs]:
-                    put(freq, values)
-                return carry
-
-            lax.fori_loop(0, NF // GROUP, body, 0)
-
         every(shifted, functools.partial(spread, wide))
         every(interacted, functools.partial(spread, quartets))
-        every(gathered, settled)
-        end = NF - 1
-        for freq, shift in ((end, -route[1, end]), (0, route[3, 0])):
-            extra = dia_coeff * quartets[home(freq, shift), :]
-            settled(freq, fresh[half, freq * ND : freq * ND + width, :] + extra)
-        save = pltpu.make_async_copy(fresh.at[half], fresh_out.at[half], out_sem.at[half])
-        save.start()
-        saves.append(save)
+        every(gathered, settled, lambda step: saving(half, step).start())
 
     def unpack_first(source, cells):
         at = PAD + source * n_chan
@@ -414,8 +430,10 @@
         return carry
 
     lax.fori_loop(1, n_spec, finish, 0)
-    for save in saves:
-        save.wait()
+    spots_save.wait()
+    for half in range(2):
+        for step in range(NF // GROUP):
+            saving(half, step).wait()
 
 
 def expand_kernel(fresh_in, spots_in, out, fresh, spots, cells, in_sem, out_sem):
@@ -487,11 +505,11 @@
             pltpu.VMEM((NF * ROWS, LANES), f32),
             pltpu.VMEM(((NF + 1) * ROWS, LANES), f32),
             pltpu.SMEM((4, NF), jnp.int32),
-            pltpu.SMEM((8, NF), jnp.int32),
+            pltpu.SMEM((9, NF), jnp.int32),
             pltpu.VMEM((2, total, LANES), f32),
             pltpu.VMEM((2 * LANES, 2 * LANES), jnp.bfloat16),
             pltpu.VMEM((LANES, 2 * LANES), f32),
-            pltpu.SemaphoreType.DMA((3,)),
+            pltpu.SemaphoreType.DMA((3, NF // GROUP)),
             pltpu.SemaphoreType.DMA((2,)),
             pltpu.SemaphoreType.DMA((2,)),
             pltpu.SemaphoreType.DMA((kinds, n_spec)),

time: 25.5 us -> 25.4 us (level)
    pallas_call x1, Pallas kernels: 22.3 us -> 22.1 us  [shards(): pl.pallas_call(functools.partial(step_kernel, packed, n_spec, n_tile, gri...]
where the time goes in v7:
time: 25.4 us; the launch traced here: 25 us
  Pallas kernels  25 us (98%)
    pallas_call x1, Pallas kernels, shards(): pl.pallas_call(functools.partial(step_kernel, packed, n_spec, n_tile, gri...  22.1 us
    pallas_call x1, Pallas kernels, shards(): pl.pallas_call(expand_kernel, out_shape=jax.ShapeDtypeStruct((total * 2,...  2.9 us

profile of v7, /device:TPU:1, one launch (start us, length us, event | category | flops | bytes accessed | tf_op | source)
XLA Modules:
  0.0 25.0 jit_solution(8199960413768779132)
XLA Ops:
  0.0 22.1 %shard_map.73 = (f32[2,1152,128]{2,1,0:T(8,128)}, bf16[256,256]{1,0:T(8,128)(2,1)}) custom-call(f32[2304,128]{1,0:T(8,128)} %bitcast.3, f32[16,128]{1,0:T(8,128)} %depth_in.1, f32[16,128]{1,0:T(8,128)} %turning_in.1, f32[1152]{0:T(1024)} %drift_in.1, s32[2,1152]{1,0:T(2,128)} %partners_in.1, s32[8,1,192]{2,1,0:T(1,128)} %slots_in.1, s32[1,8]{1,0:T(1,128)} %bitcast.4), custom_call_target="tpu_custom_call" | custom-call | tf_op jit(solution)/shard_map/pallas_call | solution.py:476
  22.1 2.9 %shard_map.74 = f32[2304,128]{1,0:T(8,128)} custom-call(f32[2,1152,128]{2,1,0:T(8,128)} %get-tuple-element.7.fresh_in, bf16[256,256]{1,0:T(8,128)(2,1)} %get-tuple-element.8.spots_in), custom_call_target="tpu_custom_call" | custom-call | tf_op jit(solution)/shard_map/pallas_call | solution.py:522

commit v8 on v7

--- a/solution.py
+++ b/solution.py
@@ -197,8 +197,16 @@
 
     last_kind = n_chan // (2 * ND) if packed else 1
 
+    def partner(step):
+        bits = [2**b for b in range(n_spec.bit_length() - 1)]
+        return sum(((me // bit) % 2 + (step // bit) % 2) % 2 * bit for bit in bits)
+
+    def turn_of(place):
+        place = place + (me % 2) * (n_spec - 2 - 2 * place)
+        return 1 + (2 * place + 1) % (n_spec - 1)
+
     def sending(kind, step):
-        peer = lax.rem(me + step, n_spec)
+        peer = partner(step)
         if kind == last_kind:
             src, dst = second.at[peer], second_in.at[me]
         elif packed:
@@ -227,20 +235,20 @@
 
     def stage(fill, kind):
         def body(group, carry):
-            steps = [BLOCKS * group + 1 + i for i in range(BLOCKS)]
-            fill([lax.rem(me + step, n_spec) for step in steps])
+            steps = [turn_of(BLOCKS * group + i) for i in range(BLOCKS)]
+            fill([partner(step) for step in steps])
             for step in steps:
                 sending(kind, step).start()
             return carry
 
         lax.fori_loop(0, n_spec // BLOCKS - 1, body, 0)
-        steps = range(n_spec - BLOCKS + 1, n_spec)
-        fill([lax.rem(me + step, n_spec) for step in steps] + [me])
+        steps = [turn_of(place) for place in range(n_spec - BLOCKS, n_spec - 1)]
+        fill([partner(step) for step in steps] + [me])
         for step in steps:
             sending(kind, step).start()
 
     def start_second(step, carry):
-        sending(last_kind, step).start()
+        sending(last_kind, turn_of(step - 1)).start()
         return carry
 
     def arrive():
@@ -403,14 +411,14 @@
         flat[pl.ds(PAD + source * count, count), :] = cells[source]
 
     def take_first(step, carry):
-        source = lax.rem(me + n_spec - step, n_spec)
+        source = partner(step)
         for kind in kinds:
             sending(kind, step).wait_recv()
         unpack_first(source, first_in)
         return carry
 
     def take_second(step, carry):
-        source = lax.rem(me + n_spec - step, n_spec)
+        source = partner(step)
         sending(last_kind, step).wait_recv()
         unpack_second(source, second_in)
         return carry

time: 25.4 us -> 25.9 us (1.020)
  Pallas kernels: 25 us -> 25.7 us
    pallas_call x1, Pallas kernels: 22.1 us -> 22.7 us  [shards(): pl.pallas_call(functools.partial(step_kernel, packed, n_spec, n_tile, gri...]
where the time goes in v8:
time: 25.9 us; the launch traced here: 25.7 us
  Pallas kernels  25.7 us (99%)
    pallas_call x1, Pallas kernels, shards(): pl.pallas_call(functools.partial(step_kernel, packed, n_spec, n_tile, gri...  22.7 us
    pallas_call x1, Pallas kernels, shards(): pl.pallas_call(expand_kernel, out_shape=jax.ShapeDtypeStruct((total * 2,...  2.9 us

profile of v8, /device:TPU:1, one launch (start us, length us, event | category | flops | bytes accessed | tf_op | source)
XLA Modules:
  0.0 25.7 jit_solution(14765961432554877567)
XLA Ops:
  0.0 22.7 %shard_map.73 = (f32[2,1152,128]{2,1,0:T(8,128)}, bf16[256,256]{1,0:T(8,128)(2,1)}) custom-call(f32[2304,128]{1,0:T(8,128)} %bitcast.3, f32[16,128]{1,0:T(8,128)} %depth_in.1, f32[16,128]{1,0:T(8,128)} %turning_in.1, f32[1152]{0:T(1024)} %drift_in.1, s32[2,1152]{1,0:T(2,128)} %partners_in.1, s32[8,1,192]{2,1,0:T(1,128)} %slots_in.1, s32[1,8]{1,0:T(1,128)} %bitcast.4), custom_call_target="tpu_custom_call" | custom-call | tf_op jit(solution)/shard_map/pallas_call | solution.py:484
  22.8 2.9 %shard_map.74 = f32[2304,128]{1,0:T(8,128)} custom-call(f32[2,1152,128]{2,1,0:T(8,128)} %get-tuple-element.7.fresh_in, bf16[256,256]{1,0:T(8,128)(2,1)} %get-tuple-element.8.spots_in), custom_call_target="tpu_custom_call" | custom-call | tf_op jit(solution)/shard_map/pallas_call | solution.py:530
